TPU v7x, 512 devices: a whole 4x8x8 slice. The times are simulated.
512 devices in a mesh: layer: 4 (over x), row: 8 (over z), col: 16 (over y, core).
Axes of the slice: x: 4, y: 8, z: 8, core: 2. Of those that a mesh axis runs over, the one named last changes fastest.
Arguments:
- a_vals: bfloat16 [4, 8, 16, 12, 128, 128], P('layer', 'row', 'col'), may hold values from -0.109375 to 0.109375
- a_rows: int32 [4, 8, 16, 12], P('layer', 'row', 'col'), may hold values from 0 to 31, as said below
- a_ks: int32 [4, 8, 16, 12], P('layer', 'row', 'col'), may hold values from 0 to 7
- a_live: int32 [4, 8, 16], P('layer', 'row', 'col'), may hold values from 6 to 12, as said below
- b_vals: bfloat16 [512, 16, 2, 128, 128], P(('layer', 'row'), 'col'), may hold values from -6 to 6
- b_cols: int32 [512, 16, 2], P(('layer', 'row'), 'col'), may hold values from 0 to 1, as said below
Outputs:
- product: float32 [128, 256, 32, 128], P('layer', 'row', 'col')
Inputs may be any that keep to these rules, and one draw needn't show every extreme that they name: On each device the pairs (a_rows, a_ks) of the 12 slots are all different. `a_live`: in every draw some device has all 12 slots live. `b_cols`: the 2 block columns of one block row and col index are all different.
All inputs are finite; a program needn't handle non-finite values.
Results may differ from a plain program's by a relative error of at most 0.0003.
Values may be sent and summed in bfloat16 or wider, within the bound.
No kernel may reach another device: no remote copies, remote signals or barrier semaphores. Data moves between devices by JAX's collectives and lax.ppermute only.
A program may use at most 64 MiB of HBM per device.

v0:
```python
import functools

import jax
import jax.numpy as jnp
from jax import lax
from jax.experimental import pallas as pl
from jax.experimental.pallas import tpu as pltpu
from jax.sharding import PartitionSpec as P

BS = 128
BLK_DEV = 8
SA = 12
PB = 2
RB_DEV = 32
CB_DEV = 2
N_LAYER = 4
N_ROW = 8
N_COL = 16
K_DEV = 16
XQ = BS // N_LAYER
A_ROWS = SA * BS
POS_ROWS = 16
MSG_ROWS = RB_DEV * XQ + RB_DEV
BITS = 13.0
LN2 = 0.6931471805599453


def piece_of(me, place):
    return lax.rem(me + place, N_ROW)


def add_products(place_ref, a_ref, places, acc, b_refs):
    row = lax.axis_index("row")
    for place, b_ref in zip(places, b_refs):

        def half(h, carry):
            col = 2 * piece_of(row, place) + h
            for s in range(SA):
                target = place_ref[col, s]
                k = place_ref[col, SA + s]
                acc[target] += jnp.dot(
                    a_ref[col, pl.ds(s * BS, BS), :],
                    b_ref[h * BLK_DEV + k],
                    preferred_element_type=jnp.float32,
                )
            return carry

        lax.fori_loop(0, 2, half, 0)


def add_both(place_ref, a_ref, places, accs, b_refs):
    row = lax.axis_index("row")
    for place, pair in zip(places, b_refs):

        def half(h, carry):
            col = 2 * piece_of(row, place) + h
            for s in range(SA):
                target = place_ref[col, s]
                k = place_ref[col, SA + s]
                block = a_ref[col, pl.ds(s * BS, BS), :]
                for acc, b_ref in zip(accs, pair):
                    acc[target] += jnp.dot(
                        block, b_ref[h * BLK_DEV + k], preferred_element_type=jnp.float32
                    )
            return carry

        lax.fori_loop(0, 2, half, 0)


def open_kernel(both, alone, resumed, place_ref, a_ref, *refs):
    width = len(alone)
    outs = refs[-width:]
    refs = list(refs[:-width])

    pairs = [[refs.pop(0) for _ in range(width)] for _ in both]
    singles = [[refs.pop(0) for _ in places] for places in alone]

    def load(i, carry):
        for c in range(width):
            outs[c][i] = refs[c][i] if resumed else jnp.zeros((BS, BS), jnp.float32)
        return carry

    lax.fori_loop(0, RB_DEV, load, 0)
    add_both(place_ref, a_ref, both, outs, pairs)
    for c in range(width):
        add_products(place_ref, a_ref, alone[c], outs[c], singles[c])


def close_kernel(places, place_ref, a_ref, *refs):
    count = len(places)
    before_ref, own_ref = refs[count : count + 2]
    msg_refs = refs[count + 2 : -2]
    acc, top = refs[-2:]
    layer = lax.axis_index("layer")

    def load(i, carry):
        acc[i] = before_ref[i]
        return carry

    lax.fori_loop(0, RB_DEV, load, 0)
    add_products(place_ref, a_ref, places, acc, refs[:count])

    def keep(i, carry):
        own_ref[i] = acc[i, pl.ds(layer * XQ, XQ), :]
        for q in range(1, N_LAYER):
            start = lax.rem(layer + q, N_LAYER) * XQ
            part = acc[i, pl.ds(start, XQ), :]
            top[q - 1, pl.ds(i, 1), :] = jnp.max(jnp.abs(part), axis=0, keepdims=True)
        return carry

    lax.fori_loop(0, RB_DEV, keep, 0)
    for q in range(1, N_LAYER):
        power = jnp.floor(jnp.log(jnp.maximum(top[q - 1], 1e-30)) * (1.0 / LN2))
        msg_refs[q - 1][pl.ds(RB_DEV * XQ, RB_DEV), :] = power.astype(jnp.int32).astype(jnp.int16)
        top[q - 1] = jnp.exp((BITS - power) * LN2)

    def pack(i, carry):
        for q in range(1, N_LAYER):
            start = lax.rem(layer + q, N_LAYER) * XQ
            part = acc[i, pl.ds(start, XQ), :] * top[q - 1, pl.ds(i, 1), :]
            msg_refs[q - 1][pl.ds(pl.multiple_of(i * XQ, XQ), XQ), :] = (
                jnp.round(part).astype(jnp.int32).astype(jnp.int16)
            )
        return carry

    lax.fori_loop(0, RB_DEV, pack, 0)


def positions_kernel(a_ref, place_ref, held, place, sem):
    copy = pltpu.make_async_copy(a_ref.at[:, pl.ds(A_ROWS, POS_ROWS)], held, sem)
    copy.start()
    copy.wait()
    for col in range(N_COL):
        place[pl.ds(col, 1), :] = held[col].astype(jnp.float32)[:1].astype(jnp.int32)
    copy = pltpu.make_async_copy(place, place_ref, sem)
    copy.start()
    copy.wait()


def positions(a_all):
    shape = (N_COL, BS)
    return pl.pallas_call(
        positions_kernel,
        out_shape=jax.ShapeDtypeStruct(shape, jnp.int32),
        in_specs=[pl.BlockSpec(memory_space=pl.ANY)],
        out_specs=pl.BlockSpec(memory_space=pltpu.SMEM),
        scratch_shapes=[
            pltpu.VMEM((N_COL, POS_ROWS, BS), jnp.bfloat16),
            pltpu.VMEM(shape, jnp.int32),
            pltpu.SemaphoreType.DMA(()),
        ],
        compiler_params=pltpu.CompilerParams(vmem_limit_bytes=50 * 2**20),
        cost_estimate=pl.CostEstimate(flops=5 * 10**9, bytes_accessed=2**20, transcendentals=0),
        name="positions",
    )(a_all)


def call_products(kernel, name, out_shape, scratch, operands, flops):
    smem = pl.BlockSpec(memory_space=pltpu.SMEM)
    vmem = pl.BlockSpec(memory_space=pltpu.VMEM)
    return pl.pallas_call(
        kernel,
        out_shape=out_shape,
        in_specs=[smem] + [vmem] * (len(operands) - 1),
        out_specs=[vmem] * len(out_shape),
        scratch_shapes=scratch,
        compiler_params=pltpu.CompilerParams(vmem_limit_bytes=6 * 2**20),
        cost_estimate=pl.CostEstimate(flops=flops, bytes_accessed=2**20, transcendentals=0),
        name=name,
    )(*operands)


def open_sums(where, chunks, both, alone, before=()):
    sums = jax.ShapeDtypeStruct((RB_DEV + 1, BS, BS), jnp.float32)
    blocks = [chunk[place] for place in both for chunk in chunks]
    blocks += [chunk[place] for chunk, places in zip(chunks, alone) for place in places]
    return call_products(
        functools.partial(open_kernel, both, alone, bool(before)),
        "open_sums",
        [sums] * len(chunks),
        [],
        [*where, *blocks, *before],
        5 * 10**9,
    )


def close_sums(where, chunk, places, before, flops):
    return call_products(
        functools.partial(close_kernel, places),
        "close_sums",
        [jax.ShapeDtypeStruct((RB_DEV, XQ, BS), jnp.float32)]
        + [jax.ShapeDtypeStruct((MSG_ROWS, BS), jnp.int16)] * (N_LAYER - 1),
        [
            pltpu.VMEM((RB_DEV + 1, BS, BS), jnp.float32),
            pltpu.VMEM((N_LAYER - 1, RB_DEV, BS), jnp.float32),
        ],
        [*where, *(chunk[place] for place in places), before],
        flops,
    )


def add_messages(own_ref, msgs, scale, i):
    total = own_ref[i]
    for q in range(N_LAYER - 1):
        part = msgs[q][pl.ds(pl.multiple_of(i * XQ, XQ), XQ), :]
        total = total + part.astype(jnp.int32).astype(jnp.float32) * scale[q, pl.ds(i, 1), :]
    return total


def load_scales(msgs, scale):
    for q in range(N_LAYER - 1):
        power = msgs[q][pl.ds(RB_DEV * XQ, RB_DEV), :].astype(jnp.int32).astype(jnp.float32)
        scale[q] = jnp.exp((power - BITS) * LN2)


def first_combine_kernel(own_ref, *refs):
    msgs, (out_ref, scale) = refs[: N_LAYER - 1], refs[N_LAYER - 1 :]
    load_scales(msgs, scale)

    def step(i, carry):
        out_ref[i] = add_messages(own_ref, msgs, scale, i)
        return carry

    lax.fori_loop(0, RB_DEV, step, 0)


def last_combine_kernel(first_ref, own_ref, *refs):
    msgs, (out_ref, scale) = refs[: N_LAYER - 1], refs[N_LAYER - 1 :]
    load_scales(msgs, scale)

    def step(i, carry):
        out_ref[pl.ds(CB_DEV * i, XQ, stride=RB_DEV * CB_DEV), :] = first_ref[i]
        out_ref[pl.ds(CB_DEV * i + 1, XQ, stride=RB_DEV * CB_DEV), :] = add_messages(own_ref, msgs, scale, i)
        return carry

    lax.fori_loop(0, RB_DEV, step, 0)


def combine(kernel, shape, parts, name):
    vmem = pl.BlockSpec(memory_space=pltpu.VMEM)
    return pl.pallas_call(
        kernel,
        out_shape=jax.ShapeDtypeStruct(shape, jnp.float32),
        in_specs=[vmem] * len(parts),
        out_specs=vmem,
        scratch_shapes=[pltpu.VMEM((N_LAYER - 1, RB_DEV, BS), jnp.float32)],
        compiler_params=pltpu.CompilerParams(vmem_limit_bytes=6 * 2**20),
        cost_estimate=pl.CostEstimate(flops=10**9, bytes_accessed=2**20, transcendentals=0),
        name=name,
    )(*parts)


def prepare_kernel(
    a_ref, rows_ref, ks_ref, live_ref, b_ref, cols_ref, a_out, zero_out, one_out, a_in, b_in, zero_in, one_in, sems
):
    load_b = pltpu.make_async_copy(b_ref, b_in, sems.at[0])
    load_a = pltpu.make_async_copy(a_ref, a_in.at[pl.ds(0, A_ROWS)], sems.at[1])
    load_b.start()
    load_a.start()
    lane = lax.broadcasted_iota(jnp.int32, (POS_ROWS, BS), 1)
    found = jnp.zeros((POS_ROWS, BS), jnp.int32)
    for s in range(SA):
        target = jnp.where(s < live_ref[0, 0, 0], rows_ref[s], RB_DEV)
        found = jnp.where(lane == s, target, found)
        found = jnp.where(lane == SA + s, ks_ref[s], found)
    a_in[pl.ds(A_ROWS, POS_ROWS), :] = found.astype(jnp.float32).astype(jnp.bfloat16)
    stores = [
        pltpu.make_async_copy(held, out, sems.at[2 + at])
        for at, (held, out) in enumerate(((zero_in, zero_out), (one_in, one_out), (a_in, a_out)))
    ]
    load_b.wait()
    for n in range(K_DEV):
        zero_in[n] = b_in[n, cols_ref[0, n]]
    stores[0].start()
    load_a.wait()
    stores[2].start()
    for n in range(K_DEV):
        one_in[n] = b_in[n, 1 - cols_ref[0, n]]
    stores[1].start()
    for store in stores:
        store.wait()


def prepare(a_vals, a_rows, a_ks, a_live, b_vals, b_cols):
    smem = pl.BlockSpec(memory_space=pltpu.SMEM)
    any_spec = pl.BlockSpec(memory_space=pl.ANY)
    a_send = jax.ShapeDtypeStruct((A_ROWS + POS_ROWS, BS), jnp.bfloat16)
    chunk = jax.ShapeDtypeStruct((K_DEV, BS, BS), jnp.bfloat16)
    return pl.pallas_call(
        prepare_kernel,
        out_shape=[a_send, chunk, chunk],
        in_specs=[any_spec, smem, smem, smem, any_spec, smem],
        out_specs=[any_spec] * 3,
        scratch_shapes=[
            pltpu.VMEM(a_send.shape, a_send.dtype),
            pltpu.VMEM((K_DEV, PB, BS, BS), jnp.bfloat16),
            pltpu.VMEM(chunk.shape, chunk.dtype),
            pltpu.VMEM(chunk.shape, chunk.dtype),
            pltpu.SemaphoreType.DMA((5,)),
        ],
        compiler_params=pltpu.CompilerParams(vmem_limit_bytes=60 * 2**20),
        name="prepare",
    )(
        a_vals.reshape(A_ROWS, BS),
        a_rows.reshape(SA),
        a_ks.reshape(SA),
        a_live,
        b_vals.reshape(K_DEV, PB, BS, BS),
        jnp.transpose(b_cols, (1, 2, 0)).reshape(PB, K_DEV),
    )


def shifted(value, axis, size, by):
    return lax.ppermute(value, axis, [(i, (i + by) % size) for i in range(size)])


def up(value):
    return shifted(value, "row", N_ROW, 1)


def down(value):
    return shifted(value, "row", N_ROW, -1)


def around(b_zero, b_one, hold, early, middle):
    zero, one = {0: b_zero}, {0: b_one}
    zero[7], one[1] = up(zero[0]), down(one[0])
    one[7], zero[1] = up(one[0]), down(zero[0])
    zero[6], one[2] = up(zero[7]), down(one[1])
    one[6], zero[2] = up(one[7]), down(zero[1])
    zero[5], one[3] = up(zero[6]), down(one[2])
    (zero[2],) = hold(zero[2])
    zero[3] = down(zero[2])
    sums = early(zero, one)
    zero[5], *sums = lax.optimization_barrier((zero[5], *sums))
    zero[4] = up(zero[5])
    sums = middle(zero, one, sums)
    one[3], one[6], *sums = lax.optimization_barrier((one[3], one[6], *sums))
    one[4], one[5] = down(one[3]), up(one[6])
    return zero, one, sums


def send_sums(parts):
    own, msgs = parts[0], parts[1:]
    sent = {q: shifted(msgs[q - 1], "layer", N_LAYER, q) for q in (2, 1, 3)}
    return [own, *sent.values()]


def body(a_vals, a_rows, a_ks, a_live, b_vals, b_cols):
    a_send, b_zero, b_one = prepare(a_vals, a_rows, a_ks, a_live, b_vals, b_cols)
    a_all = lax.all_gather(a_send, "col", axis=0)
    where = [positions(a_all), a_all]

    def hold(*behind):
        *behind, where[0] = lax.optimization_barrier((*behind, where[0]))
        return behind

    def early(zero, one):
        return open_sums(where, (zero, one), (7, 1), ((), ()))

    def middle(zero, one, sums):
        return open_sums(where, (zero, one), (6, 2, 0), ((5,), (3,)), sums)

    zero, one, sums = around(b_zero, b_one, hold, early, middle)
    before = open_sums(where, (zero,), (), ((3,),), sums[:1])
    parts = send_sums(close_sums(where, zero, (4,), before[0], 2 * 10**10))
    first = combine(first_combine_kernel, (RB_DEV, XQ, BS), parts, "first_combine")
    parts = send_sums(close_sums(where, one, (4, 5), sums[1], 10**11))
    rows = XQ * RB_DEV * CB_DEV
    product = combine(last_combine_kernel, (rows, BS), [first] + parts, "last_combine")
    return product.reshape(XQ, RB_DEV, CB_DEV, BS)


def solution(mesh):
    return jax.shard_map(
        body,
        mesh=mesh,
        in_specs=(
            P("layer", "row", "col", None, None, None),
            P("layer", "row", "col", None),
            P("layer", "row", "col", None),
            P("layer", "row", "col"),
            P(("layer", "row"), "col", None, None, None),
            P(("layer", "row"), "col", None),
        ),
        out_specs=P("layer", "row", "col", None),
        check_vma=False,
    )
```

profile of v0, /device:TPU:1, one launch (start us, length us, event | category | flops | bytes accessed | tf_op | source)
XLA Modules:
  0.0 134.1 jit_solution(3567331809137586370)
XLA Ops:
  7.2 3.1 %prepare.1 = (bf16[1552,128]{1,0:T(8,128)(2,1)}, bf16[16,128,128]{2,1,0:T(8,128)(2,1)}, bf16[16,128,128]{2,1,0:T(8,128)(2,1)}) custom-call(bf16[1536,128]{1,0:T(8,128)(2,1)} %bitcast.16, s32[12]{0:T(128)} %bitcast.18, s32[12]{0:T(128)} %bitcast.19, s32[1,1,1]{2,1,0:T(1,128)S(6)} %copy.7.live_ref, bf16[16,2,128,128]{3,2,1,0:T(8,128)(2,1)} %bitcast.15, ...), custom_call_target="tpu_custom_call" | custom-call | tf_op jit(solution)/shard_map/prepare/pallas_call | solution.py:289
  10.3 0.0 all-gather.3.cloned.1.call-update
  10.3 4.9 %collective-permute-start.2 = (bf16[16,128,128]{2,1,0:T(8,128)(2,1)}, bf16[16,128,128]{2,1,0:T(8,128)(2,1)S(1)}, u32[]{:S(2)}, u32[]{:S(2)}) collective-permute-start(bf16[16,128,128]{2,1,0:T(8,128)(2,1)} %get-tuple-element.29.refs_4_), channel_id=1, source_target_pairs={{0,16},{16,32},{32,48},{48,64},{64,80},{80,96},{96,112},{112,0},{1... | collective-permute-start | bytes 1572872 | tf_op jit(solution)/shard_map/ppermute | solution.py:314
  15.2 8.6 %collective-permute-start.6 = (bf16[16,128,128]{2,1,0:T(8,128)(2,1)}, bf16[16,128,128]{2,1,0:T(8,128)(2,1)S(1)}, u32[]{:S(2)}, u32[]{:S(2)}) collective-permute-start(bf16[16,128,128]{2,1,0:T(8,128)(2,1)} %get-tuple-element.32.refs_5_), channel_id=1, source_target_pairs={{0,112},{16,0},{32,16},{48,32},{64,48},{80,64},{96,80},{112,96},{1... | collective-permute-start | bytes 1572872 | tf_op jit(solution)/shard_map/ppermute | solution.py:314
  23.8 3.4 %collective-permute-start = (bf16[16,128,128]{2,1,0:T(8,128)(2,1)}, bf16[16,128,128]{2,1,0:T(8,128)(2,1)}, u32[]{:S(2)}, u32[]{:S(2)}) collective-permute-start(bf16[16,128,128]{2,1,0:T(8,128)(2,1)} %get-tuple-element.29.refs_4_), channel_id=1, source_target_pairs={{0,112},{16,0},{32,16},{48,32},{64,48},{80,64},{96,80},{112,96},{1... | collective-permute-start | bytes 1572872 | tf_op jit(solution)/shard_map/ppermute | solution.py:314
  27.1 1.9 %collective-permute-start.5 = (bf16[16,128,128]{2,1,0:T(8,128)(2,1)}, bf16[16,128,128]{2,1,0:T(8,128)(2,1)S(1)}, u32[]{:S(2)}, u32[]{:S(2)}) collective-permute-start(bf16[16,128,128]{2,1,0:T(8,128)(2,1)} %get-tuple-element.32.refs_5_), channel_id=1, source_target_pairs={{0,16},{16,32},{32,48},{48,64},{64,80},{80,96},{96,112},{112,0},{1... | collective-permute-start | bytes 1572872 | tf_op jit(solution)/shard_map/ppermute | solution.py:314
  29.1 4.6 %collective-permute-done.2.refs_0_ = bf16[16,128,128]{2,1,0:T(8,128)(2,1)S(1)} collective-permute-done((bf16[16,128,128]{2,1,0:T(8,128)(2,1)}, bf16[16,128,128]{2,1,0:T(8,128)(2,1)S(1)}, u32[]{:S(2)}, u32[]{:S(2)}) %collective-permute-start.2) | collective-permute-done | bytes 524320 | tf_op jit(solution)/shard_map/ppermute | solution.py:314
  33.7 1.9 %collective-permute-start.3 = (bf16[16,128,128]{2,1,0:T(8,128)(2,1)S(1)}, bf16[16,128,128]{2,1,0:T(8,128)(2,1)S(1)}, u32[]{:S(2)}, u32[]{:S(2)}) collective-permute-start(bf16[16,128,128]{2,1,0:T(8,128)(2,1)S(1)} %collective-permute-done.2.refs_0_), channel_id=1, source_target_pairs={{0,16},{16,32},{32,48},{48,64},{64,80},{80,96},{96,112},{112,0},{1... | collective-permute-start | bytes 1572872 | tf_op jit(solution)/shard_map/ppermute | solution.py:314
  35.6 0.0 collective-permute-done.6.refs_3_
  35.6 4.6 %collective-permute-start.9 = (bf16[16,128,128]{2,1,0:T(8,128)(2,1)S(1)}, bf16[16,128,128]{2,1,0:T(8,128)(2,1)}, u32[]{:S(2)}, u32[]{:S(2)}) collective-permute-start(bf16[16,128,128]{2,1,0:T(8,128)(2,1)S(1)} %collective-permute-done.6.refs_3_), channel_id=1, source_target_pairs={{0,112},{16,0},{32,16},{48,32},{64,48},{80,64},{96,80},{112,96},{1... | collective-permute-start | bytes 1572872 | tf_op jit(solution)/shard_map/ppermute | solution.py:314
  40.2 0.8 copy-done.3
  41.0 4.9 %collective-permute-done.refs_2_ = bf16[16,128,128]{2,1,0:T(8,128)(2,1)} collective-permute-done((bf16[16,128,128]{2,1,0:T(8,128)(2,1)}, bf16[16,128,128]{2,1,0:T(8,128)(2,1)}, u32[]{:S(2)}, u32[]{:S(2)}) %collective-permute-start) | collective-permute-done | bytes 524320 | tf_op jit(solution)/shard_map/ppermute | solution.py:314
  45.9 5.3 %collective-permute-start.1 = (bf16[16,128,128]{2,1,0:T(8,128)(2,1)}, bf16[16,128,128]{2,1,0:T(8,128)(2,1)S(1)}, u32[]{:S(2)}, u32[]{:S(2)}) collective-permute-start(bf16[16,128,128]{2,1,0:T(8,128)(2,1)} %collective-permute-done.refs_2_), channel_id=1, source_target_pairs={{0,112},{16,0},{32,16},{48,32},{64,48},{80,64},{96,80},{112,96},{1... | collective-permute-start | bytes 1572872 | tf_op jit(solution)/shard_map/ppermute | solution.py:314
  51.2 0.0 collective-permute-done.5.refs_1_
  51.2 1.9 %collective-permute-start.11 = (bf16[16,128,128]{2,1,0:T(8,128)(2,1)S(1)}, bf16[16,128,128]{2,1,0:T(8,128)(2,1)S(1)}, u32[]{:S(2)}, u32[]{:S(2)}) collective-permute-start(bf16[16,128,128]{2,1,0:T(8,128)(2,1)S(1)} %collective-permute-done.5.refs_1_), channel_id=1, source_target_pairs={{0,16},{16,32},{32,48},{48,64},{64,80},{80,96},{96,112},{112,0},{1... | collective-permute-start | bytes 1572872 | tf_op jit(solution)/shard_map/ppermute | solution.py:314
  53.1 3.1 %collective-permute-done.3.refs_0_ = bf16[16,128,128]{2,1,0:T(8,128)(2,1)S(1)} collective-permute-done((bf16[16,128,128]{2,1,0:T(8,128)(2,1)S(1)}, bf16[16,128,128]{2,1,0:T(8,128)(2,1)S(1)}, u32[]{:S(2)}, u32[]{:S(2)}) %collective-permute-start.3) | collective-permute-done | bytes 524320 | tf_op jit(solution)/shard_map/ppermute | solution.py:314
  56.3 1.9 %collective-permute-start.4 = (bf16[16,128,128]{2,1,0:T(8,128)(2,1)S(1)}, bf16[16,128,128]{2,1,0:T(8,128)(2,1)}, u32[]{:S(2)}, u32[]{:S(2)}) collective-permute-start(bf16[16,128,128]{2,1,0:T(8,128)(2,1)S(1)} %collective-permute-done.3.refs_0_), channel_id=1, source_target_pairs={{0,16},{16,32},{32,48},{48,64},{64,80},{80,96},{96,112},{112,0},{1... | collective-permute-start | bytes 1572872 | tf_op jit(solution)/shard_map/ppermute | solution.py:314
  58.2 0.0 collective-permute-done.9.refs_3_
  58.2 4.6 %collective-permute-start.10 = (bf16[16,128,128]{2,1,0:T(8,128)(2,1)}, bf16[16,128,128]{2,1,0:T(8,128)(2,1)S(1)}, u32[]{:S(2)}, u32[]{:S(2)}) collective-permute-start(bf16[16,128,128]{2,1,0:T(8,128)(2,1)} %collective-permute-done.9.refs_3_), channel_id=1, source_target_pairs={{0,112},{16,0},{32,16},{48,32},{64,48},{80,64},{96,80},{112,96},{1... | collective-permute-start | bytes 1572872 | tf_op jit(solution)/shard_map/ppermute | solution.py:314
  62.8 2.3 %all-gather.3.cloned.1.call-done = bf16[24832,128]{1,0:T(8,128)(2,1)} async-done(((bf16[1552,128]{1,0:T(8,128)(2,1)}), bf16[24832,128]{1,0:T(8,128)(2,1)}) %all-gather.3.cloned.1.call-update) | async-done | bytes 6357008 | tf_op jit(solution)/shard_map/all_gather | solution.py:351
  65.1 2.4 %positions.1.place_ref = s32[16,128]{1,0:T(8,128)S(1)} custom-call(bf16[16,1552,128]{2,1,0:T(8,128)(2,1)} %bitcast.9), custom_call_target="tpu_custom_call" | custom-call | flops 5000000000 | bytes 1048576 | tf_op jit(solution)/shard_map/positions/pallas_call | solution.py:142
  67.5 0.0 copy-start.1
  67.5 0.8 collective-permute-done.1.refs_2_
  68.4 5.2 %collective-permute-start.8 = (bf16[16,128,128]{2,1,0:T(8,128)(2,1)S(1)}, bf16[16,128,128]{2,1,0:T(8,128)(2,1)S(1)}, u32[]{:S(2)}, u32[]{:S(2)}) collective-permute-start(bf16[16,128,128]{2,1,0:T(8,128)(2,1)S(1)} %collective-permute-done.1.refs_2_), channel_id=1, source_target_pairs={{0,112},{16,0},{32,16},{48,32},{64,48},{80,64},{96,80},{112,96},{1... | collective-permute-start | bytes 1572872 | tf_op jit(solution)/shard_map/ppermute | solution.py:314
  73.6 2.9 %open_sums.3 = (f32[33,128,128]{2,1,0:T(8,128)S(1)}, f32[33,128,128]{2,1,0:T(8,128)S(1)}) custom-call(s32[16,128]{1,0:T(8,128)S(1)} %positions.1.place_ref, bf16[16,1552,128]{2,1,0:T(8,128)(2,1)S(1)} %bitcast.10, bf16[16,128,128]{2,1,0:T(8,128)(2,1)S(1)} %collective-permute-done.2.refs_0_, bf16[16,128,128]{2,1,0:T(8,128)(2,1)S(1)} %collective-permute-done.5.refs_1_, ...), custom_call_target="tpu_custom_call" | custom-call | flops 5000000000 | bytes 1048576 | tf_op jit(solution)/shard_map/open_sums/pallas_call | solution.py:161
  76.5 1.9 %collective-permute-start.7 = (bf16[16,128,128]{2,1,0:T(8,128)(2,1)}, bf16[16,128,128]{2,1,0:T(8,128)(2,1)S(1)}, u32[]{:S(2)}, u32[]{:S(2)}) collective-permute-start(bf16[16,128,128]{2,1,0:T(8,128)(2,1)} %collective-permute-done.4.refs_6_), channel_id=1, source_target_pairs={{0,16},{16,32},{32,48},{48,64},{64,80},{80,96},{96,112},{112,0},{1... | collective-permute-start | bytes 1572872 | tf_op jit(solution)/shard_map/ppermute | solution.py:314
  78.5 1.1 collective-permute-done.10.refs_7_
  79.6 4.9 %open_sums.4 = (f32[33,128,128]{2,1,0:T(8,128)S(1)}, f32[33,128,128]{2,1,0:T(8,128)S(1)}) custom-call(s32[16,128]{1,0:T(8,128)S(1)} %positions.1.place_ref, bf16[16,1552,128]{2,1,0:T(8,128)(2,1)S(1)} %bitcast.11, bf16[16,128,128]{2,1,0:T(8,128)(2,1)S(1)} %collective-permute-done.3.refs_0_, bf16[16,128,128]{2,1,0:T(8,128)(2,1)S(1)} %collective-permute-done.11.refs_1_, ...), custom_call_target="tpu_custom_call" | custom-call | flops 5000000000 | bytes 1048576 | tf_op jit(solution)/shard_map/open_sums/pallas_call | solution.py:161
  84.5 5.2 %collective-permute-start.15 = (bf16[16,128,128]{2,1,0:T(8,128)(2,1)S(1)}, bf16[16,128,128]{2,1,0:T(8,128)(2,1)S(1)}, u32[]{:S(2)}, u32[]{:S(2)}) collective-permute-start(bf16[16,128,128]{2,1,0:T(8,128)(2,1)S(1)} %collective-permute-done.10.refs_7_), channel_id=1, source_target_pairs={{0,112},{16,0},{32,16},{48,32},{64,48},{80,64},{96,80},{112,96},{1... | collective-permute-start | bytes 1572872 | tf_op jit(solution)/shard_map/ppermute | solution.py:314
  89.8 1.9 %collective-permute-start.16 = (bf16[16,128,128]{2,1,0:T(8,128)(2,1)S(1)}, bf16[16,128,128]{2,1,0:T(8,128)(2,1)S(1)}, u32[]{:S(2)}, u32[]{:S(2)}) collective-permute-start(bf16[16,128,128]{2,1,0:T(8,128)(2,1)S(1)} %collective-permute-done.11.refs_1_), channel_id=1, source_target_pairs={{0,16},{16,32},{32,48},{48,64},{64,80},{80,96},{96,112},{112,0},{1... | collective-permute-start | bytes 1572872 | tf_op jit(solution)/shard_map/ppermute | solution.py:314
  91.7 0.0 collective-permute-done.8.refs_0_
  91.7 1.4 %open_sums.5.refs_1_ = f32[33,128,128]{2,1,0:T(8,128)S(1)} custom-call(s32[16,128]{1,0:T(8,128)S(1)} %positions.1.place_ref, bf16[16,1552,128]{2,1,0:T(8,128)(2,1)S(1)} %bitcast.12, bf16[16,128,128]{2,1,0:T(8,128)(2,1)S(1)} %collective-permute-done.8.refs_0_, f32[33,128,128]{2,1,0:T(8,128)S(1)} %get-tuple-element.41.refs_1_), custom_call_target="tpu_custom_call" | custom-call | flops 5000000000 | bytes 1048576 | tf_op jit(solution)/shard_map/open_sums/pallas_call | solution.py:161
  93.1 0.0 collective-permute-done.7.refs_0_
  93.1 2.4 %close_sums.2 = (f32[32,32,128]{2,1,0:T(8,128)S(1)}, s16[1056,128]{1,0:T(8,128)(2,1)S(1)}, s16[1056,128]{1,0:T(8,128)(2,1)S(1)}, s16[1056,128]{1,0:T(8,128)(2,1)S(1)}) custom-call(s32[16,128]{1,0:T(8,128)S(1)} %positions.1.place_ref, bf16[16,1552,128]{2,1,0:T(8,128)(2,1)S(1)} %bitcast.13, bf16[16,128,128]{2,1,0:T(8,128)(2,1)S(1)} %collective-permute-done.7.refs_0_, ...), custom_call_target="tpu_custom_call" | custom-call | flops 20000000000 | bytes 1048576 | tf_op jit(solution)/shard_map/close_sums/pallas_call | solution.py:161
  95.6 4.7 %collective-permute-start.12 = (s16[1056,128]{1,0:T(8,128)(2,1)S(1)}, s16[1056,128]{1,0:T(8,128)(2,1)S(1)}, u32[]{:S(2)}, u32[]{:S(2)}) collective-permute-start(s16[1056,128]{1,0:T(8,128)(2,1)S(1)} %get-tuple-element.43), channel_id=1, source_target_pairs={{0,256},{128,384},{256,0},{384,128},{1,257},{129,385},{257,1},{385... | collective-permute-start | bytes 811016 | tf_op jit(solution)/shard_map/ppermute | solution.py:314
  100.2 2.2 %collective-permute-start.13 = (s16[1056,128]{1,0:T(8,128)(2,1)S(1)}, s16[1056,128]{1,0:T(8,128)(2,1)S(1)}, u32[]{:S(2)}, u32[]{:S(2)}) collective-permute-start(s16[1056,128]{1,0:T(8,128)(2,1)S(1)} %get-tuple-element.44), channel_id=1, source_target_pairs={{0,128},{128,256},{256,384},{384,0},{1,129},{129,257},{257,385},{3... | collective-permute-start | bytes 811016 | tf_op jit(solution)/shard_map/ppermute | solution.py:314
  102.5 4.3 %collective-permute-start.14 = (s16[1056,128]{1,0:T(8,128)(2,1)S(1)}, s16[1056,128]{1,0:T(8,128)(2,1)S(1)}, u32[]{:S(2)}, u32[]{:S(2)}) collective-permute-start(s16[1056,128]{1,0:T(8,128)(2,1)S(1)} %get-tuple-element.45), channel_id=1, source_target_pairs={{0,384},{128,0},{256,128},{384,256},{1,385},{129,1},{257,129},{385... | collective-permute-start | bytes 811016 | tf_op jit(solution)/shard_map/ppermute | solution.py:314
  106.8 0.0 collective-permute-done.16.refs_1_
  106.8 3.0 %close_sums.3 = (f32[32,32,128]{2,1,0:T(8,128)S(1)}, s16[1056,128]{1,0:T(8,128)(2,1)S(1)}, s16[1056,128]{1,0:T(8,128)(2,1)S(1)}, s16[1056,128]{1,0:T(8,128)(2,1)S(1)}) custom-call(s32[16,128]{1,0:T(8,128)S(1)} %positions.1.place_ref, bf16[16,1552,128]{2,1,0:T(8,128)(2,1)S(1)} %bitcast.14, bf16[16,128,128]{2,1,0:T(8,128)(2,1)S(1)} %collective-permute-done.15.refs_0_, ...), custom_call_target="tpu_custom_call" | custom-call | flops 99999997952 | bytes 1048576 | tf_op jit(solution)/shard_map/close_sums/pallas_call | solution.py:161
  109.8 1.9 %collective-permute-start.17 = (s16[1056,128]{1,0:T(8,128)(2,1)S(1)}, s16[1056,128]{1,0:T(8,128)(2,1)S(1)}, u32[]{:S(2)}, u32[]{:S(2)}) collective-permute-start(s16[1056,128]{1,0:T(8,128)(2,1)S(1)} %get-tuple-element.50), channel_id=1, source_target_pairs={{0,256},{128,384},{256,0},{384,128},{1,257},{129,385},{257,1},{385... | collective-permute-start | bytes 811016 | tf_op jit(solution)/shard_map/ppermute | solution.py:314
  111.7 2.5 %collective-permute-start.18 = (s16[1056,128]{1,0:T(8,128)(2,1)S(1)}, s16[1056,128]{1,0:T(8,128)(2,1)S(1)}, u32[]{:S(2)}, u32[]{:S(2)}) collective-permute-start(s16[1056,128]{1,0:T(8,128)(2,1)S(1)} %get-tuple-element.51), channel_id=1, source_target_pairs={{0,128},{128,256},{256,384},{384,0},{1,129},{129,257},{257,385},{3... | collective-permute-start | bytes 811016 | tf_op jit(solution)/shard_map/ppermute | solution.py:314
  114.2 4.0 %collective-permute-start.19 = (s16[1056,128]{1,0:T(8,128)(2,1)S(1)}, s16[1056,128]{1,0:T(8,128)(2,1)S(1)}, u32[]{:S(2)}, u32[]{:S(2)}) collective-permute-start(s16[1056,128]{1,0:T(8,128)(2,1)S(1)} %get-tuple-element.52), channel_id=1, source_target_pairs={{0,384},{128,0},{256,128},{384,256},{1,385},{129,1},{257,129},{385... | collective-permute-start | bytes 811016 | tf_op jit(solution)/shard_map/ppermute | solution.py:314
  118.2 0.0 collective-permute-done.13.refs_1_
  118.2 0.0 collective-permute-done.14.refs_2_
  118.2 0.4 first_combine.1.first_ref
  118.7 6.5 %collective-permute-done.18.refs_1_ = s16[1056,128]{1,0:T(8,128)(2,1)S(1)} collective-permute-done((s16[1056,128]{1,0:T(8,128)(2,1)S(1)}, s16[1056,128]{1,0:T(8,128)(2,1)S(1)}, u32[]{:S(2)}, u32[]{:S(2)}) %collective-permute-start.18) | collective-permute-done | bytes 270368 | tf_op jit(solution)/shard_map/ppermute | solution.py:314
  125.1 0.0 collective-permute-done.19.refs_2_
  125.1 2.1 %last_combine.1 = f32[2048,128]{1,0:T(8,128)} custom-call(f32[32,32,128]{2,1,0:T(8,128)S(1)} %first_combine.1.first_ref, f32[32,32,128]{2,1,0:T(8,128)S(1)} %get-tuple-element.49.own_ref, s16[1056,128]{1,0:T(8,128)(2,1)S(1)} %collective-permute-done.17.refs_0_, s16[1056,128]{1,0:T(8,128)(2,1)S(1)} %collective-permute-done.18.refs_1_, ...), custom_call_target="tpu_custom_call" | custom-call | flops 1000000000 | bytes 1048576 | tf_op jit(solution)/shard_map/last_combine/pallas_call | solution.py:241
  (14 shorter events, 0.0 us)
Async XLA Ops:
  6.5 58.6 %all-gather.3.cloned.1.call-start = ((), (), s32[]{:S(2)}) async-start(), calls=%async_computation | async-start | bytes 6754304 | tf_op jit(solution)/shard_map/all_gather | solution.py:351
  10.3 23.3 %collective-permute-start.2 = (bf16[16,128,128]{2,1,0:T(8,128)(2,1)}, bf16[16,128,128]{2,1,0:T(8,128)(2,1)S(1)}, u32[]{:S(2)}, u32[]{:S(2)}) collective-permute-start(bf16[16,128,128]{2,1,0:T(8,128)(2,1)} %get-tuple-element.29.refs_4_), channel_id=1, source_target_pairs={{0,16},{16,32},{32,48},{48,64},{64,80},{80,96},{96,112},{112,0},{1... | collective-permute-start | bytes 1572872 | tf_op jit(solution)/shard_map/ppermute | solution.py:314
  15.2 20.4 %collective-permute-start.6 = (bf16[16,128,128]{2,1,0:T(8,128)(2,1)}, bf16[16,128,128]{2,1,0:T(8,128)(2,1)S(1)}, u32[]{:S(2)}, u32[]{:S(2)}) collective-permute-start(bf16[16,128,128]{2,1,0:T(8,128)(2,1)} %get-tuple-element.32.refs_5_), channel_id=1, source_target_pairs={{0,112},{16,0},{32,16},{48,32},{64,48},{80,64},{96,80},{112,96},{1... | collective-permute-start | bytes 1572872 | tf_op jit(solution)/shard_map/ppermute | solution.py:314
  23.8 22.1 %collective-permute-start = (bf16[16,128,128]{2,1,0:T(8,128)(2,1)}, bf16[16,128,128]{2,1,0:T(8,128)(2,1)}, u32[]{:S(2)}, u32[]{:S(2)}) collective-permute-start(bf16[16,128,128]{2,1,0:T(8,128)(2,1)} %get-tuple-element.29.refs_4_), channel_id=1, source_target_pairs={{0,112},{16,0},{32,16},{48,32},{64,48},{80,64},{96,80},{112,96},{1... | collective-permute-start | bytes 1572872 | tf_op jit(solution)/shard_map/ppermute | solution.py:314
  27.1 24.1 %collective-permute-start.5 = (bf16[16,128,128]{2,1,0:T(8,128)(2,1)}, bf16[16,128,128]{2,1,0:T(8,128)(2,1)S(1)}, u32[]{:S(2)}, u32[]{:S(2)}) collective-permute-start(bf16[16,128,128]{2,1,0:T(8,128)(2,1)} %get-tuple-element.32.refs_5_), channel_id=1, source_target_pairs={{0,16},{16,32},{32,48},{48,64},{64,80},{80,96},{96,112},{112,0},{1... | collective-permute-start | bytes 1572872 | tf_op jit(solution)/shard_map/ppermute | solution.py:314
  33.7 22.6 %collective-permute-start.3 = (bf16[16,128,128]{2,1,0:T(8,128)(2,1)S(1)}, bf16[16,128,128]{2,1,0:T(8,128)(2,1)S(1)}, u32[]{:S(2)}, u32[]{:S(2)}) collective-permute-start(bf16[16,128,128]{2,1,0:T(8,128)(2,1)S(1)} %collective-permute-done.2.refs_0_), channel_id=1, source_target_pairs={{0,16},{16,32},{32,48},{48,64},{64,80},{80,96},{96,112},{112,0},{1... | collective-permute-start | bytes 1572872 | tf_op jit(solution)/shard_map/ppermute | solution.py:314
  35.6 22.6 %collective-permute-start.9 = (bf16[16,128,128]{2,1,0:T(8,128)(2,1)S(1)}, bf16[16,128,128]{2,1,0:T(8,128)(2,1)}, u32[]{:S(2)}, u32[]{:S(2)}) collective-permute-start(bf16[16,128,128]{2,1,0:T(8,128)(2,1)S(1)} %collective-permute-done.6.refs_3_), channel_id=1, source_target_pairs={{0,112},{16,0},{32,16},{48,32},{64,48},{80,64},{96,80},{112,96},{1... | collective-permute-start | bytes 1572872 | tf_op jit(solution)/shard_map/ppermute | solution.py:314
  40.2 0.8 copy-start.3
  45.9 22.5 %collective-permute-start.1 = (bf16[16,128,128]{2,1,0:T(8,128)(2,1)}, bf16[16,128,128]{2,1,0:T(8,128)(2,1)S(1)}, u32[]{:S(2)}, u32[]{:S(2)}) collective-permute-start(bf16[16,128,128]{2,1,0:T(8,128)(2,1)} %collective-permute-done.refs_2_), channel_id=1, source_target_pairs={{0,112},{16,0},{32,16},{48,32},{64,48},{80,64},{96,80},{112,96},{1... | collective-permute-start | bytes 1572872 | tf_op jit(solution)/shard_map/ppermute | solution.py:314
  51.2 27.2 %collective-permute-start.11 = (bf16[16,128,128]{2,1,0:T(8,128)(2,1)S(1)}, bf16[16,128,128]{2,1,0:T(8,128)(2,1)S(1)}, u32[]{:S(2)}, u32[]{:S(2)}) collective-permute-start(bf16[16,128,128]{2,1,0:T(8,128)(2,1)S(1)} %collective-permute-done.5.refs_1_), channel_id=1, source_target_pairs={{0,16},{16,32},{32,48},{48,64},{64,80},{80,96},{96,112},{112,0},{1... | collective-permute-start | bytes 1572872 | tf_op jit(solution)/shard_map/ppermute | solution.py:314
  56.3 20.2 %collective-permute-start.4 = (bf16[16,128,128]{2,1,0:T(8,128)(2,1)S(1)}, bf16[16,128,128]{2,1,0:T(8,128)(2,1)}, u32[]{:S(2)}, u32[]{:S(2)}) collective-permute-start(bf16[16,128,128]{2,1,0:T(8,128)(2,1)S(1)} %collective-permute-done.3.refs_0_), channel_id=1, source_target_pairs={{0,16},{16,32},{32,48},{48,64},{64,80},{80,96},{96,112},{112,0},{1... | collective-permute-start | bytes 1572872 | tf_op jit(solution)/shard_map/ppermute | solution.py:314
  58.2 21.4 %collective-permute-start.10 = (bf16[16,128,128]{2,1,0:T(8,128)(2,1)}, bf16[16,128,128]{2,1,0:T(8,128)(2,1)S(1)}, u32[]{:S(2)}, u32[]{:S(2)}) collective-permute-start(bf16[16,128,128]{2,1,0:T(8,128)(2,1)} %collective-permute-done.9.refs_3_), channel_id=1, source_target_pairs={{0,112},{16,0},{32,16},{48,32},{64,48},{80,64},{96,80},{112,96},{1... | collective-permute-start | bytes 1572872 | tf_op jit(solution)/shard_map/ppermute | solution.py:314
  65.1 8.5 %copy-start = (bf16[24832,128]{1,0:T(8,128)(2,1)S(1)}, bf16[24832,128]{1,0:T(8,128)(2,1)}, u32[]{:S(2)}) copy-start(bf16[24832,128]{1,0:T(8,128)(2,1)} %all-gather.3.cloned.1.call-done) | copy-start | bytes 19070980
  65.1 8.5 %copy-start.4 = (bf16[16,128,128]{2,1,0:T(8,128)(2,1)S(1)}, bf16[16,128,128]{2,1,0:T(8,128)(2,1)}, u32[]{:S(2)}) copy-start(bf16[16,128,128]{2,1,0:T(8,128)(2,1)} %copy-done.3) | copy-start | bytes 1572868
  67.5 12.1 %copy-start.1 = (bf16[16,128,128]{2,1,0:T(8,128)(2,1)S(1)}, bf16[16,128,128]{2,1,0:T(8,128)(2,1)}, u32[]{:S(2)}) copy-start(bf16[16,128,128]{2,1,0:T(8,128)(2,1)} %get-tuple-element.29.refs_4_) | copy-start | bytes 1572868
  67.5 12.1 %copy-start.2 = (bf16[16,128,128]{2,1,0:T(8,128)(2,1)S(1)}, bf16[16,128,128]{2,1,0:T(8,128)(2,1)}, u32[]{:S(2)}) copy-start(bf16[16,128,128]{2,1,0:T(8,128)(2,1)} %get-tuple-element.32.refs_5_) | copy-start | bytes 1572868
  68.4 23.3 %collective-permute-start.8 = (bf16[16,128,128]{2,1,0:T(8,128)(2,1)S(1)}, bf16[16,128,128]{2,1,0:T(8,128)(2,1)S(1)}, u32[]{:S(2)}, u32[]{:S(2)}) collective-permute-start(bf16[16,128,128]{2,1,0:T(8,128)(2,1)S(1)} %collective-permute-done.1.refs_2_), channel_id=1, source_target_pairs={{0,112},{16,0},{32,16},{48,32},{64,48},{80,64},{96,80},{112,96},{1... | collective-permute-start | bytes 1572872 | tf_op jit(solution)/shard_map/ppermute | solution.py:314
  76.5 16.6 %collective-permute-start.7 = (bf16[16,128,128]{2,1,0:T(8,128)(2,1)}, bf16[16,128,128]{2,1,0:T(8,128)(2,1)S(1)}, u32[]{:S(2)}, u32[]{:S(2)}) collective-permute-start(bf16[16,128,128]{2,1,0:T(8,128)(2,1)} %collective-permute-done.4.refs_6_), channel_id=1, source_target_pairs={{0,16},{16,32},{32,48},{48,64},{64,80},{80,96},{96,112},{112,0},{1... | collective-permute-start | bytes 1572872 | tf_op jit(solution)/shard_map/ppermute | solution.py:314
  84.5 22.2 %collective-permute-start.15 = (bf16[16,128,128]{2,1,0:T(8,128)(2,1)S(1)}, bf16[16,128,128]{2,1,0:T(8,128)(2,1)S(1)}, u32[]{:S(2)}, u32[]{:S(2)}) collective-permute-start(bf16[16,128,128]{2,1,0:T(8,128)(2,1)S(1)} %collective-permute-done.10.refs_7_), channel_id=1, source_target_pairs={{0,112},{16,0},{32,16},{48,32},{64,48},{80,64},{96,80},{112,96},{1... | collective-permute-start | bytes 1572872 | tf_op jit(solution)/shard_map/ppermute | solution.py:314
  89.8 17.0 %collective-permute-start.16 = (bf16[16,128,128]{2,1,0:T(8,128)(2,1)S(1)}, bf16[16,128,128]{2,1,0:T(8,128)(2,1)S(1)}, u32[]{:S(2)}, u32[]{:S(2)}) collective-permute-start(bf16[16,128,128]{2,1,0:T(8,128)(2,1)S(1)} %collective-permute-done.11.refs_1_), channel_id=1, source_target_pairs={{0,16},{16,32},{32,48},{48,64},{64,80},{80,96},{96,112},{112,0},{1... | collective-permute-start | bytes 1572872 | tf_op jit(solution)/shard_map/ppermute | solution.py:314
  95.6 18.6 %collective-permute-start.12 = (s16[1056,128]{1,0:T(8,128)(2,1)S(1)}, s16[1056,128]{1,0:T(8,128)(2,1)S(1)}, u32[]{:S(2)}, u32[]{:S(2)}) collective-permute-start(s16[1056,128]{1,0:T(8,128)(2,1)S(1)} %get-tuple-element.43), channel_id=1, source_target_pairs={{0,256},{128,384},{256,0},{384,128},{1,257},{129,385},{257,1},{385... | collective-permute-start | bytes 811016 | tf_op jit(solution)/shard_map/ppermute | solution.py:314
  100.2 18.0 %collective-permute-start.13 = (s16[1056,128]{1,0:T(8,128)(2,1)S(1)}, s16[1056,128]{1,0:T(8,128)(2,1)S(1)}, u32[]{:S(2)}, u32[]{:S(2)}) collective-permute-start(s16[1056,128]{1,0:T(8,128)(2,1)S(1)} %get-tuple-element.44), channel_id=1, source_target_pairs={{0,128},{128,256},{256,384},{384,0},{1,129},{129,257},{257,385},{3... | collective-permute-start | bytes 811016 | tf_op jit(solution)/shard_map/ppermute | solution.py:314
  102.5 15.8 %collective-permute-start.14 = (s16[1056,128]{1,0:T(8,128)(2,1)S(1)}, s16[1056,128]{1,0:T(8,128)(2,1)S(1)}, u32[]{:S(2)}, u32[]{:S(2)}) collective-permute-start(s16[1056,128]{1,0:T(8,128)(2,1)S(1)} %get-tuple-element.45), channel_id=1, source_target_pairs={{0,384},{128,0},{256,128},{384,256},{1,385},{129,1},{257,129},{385... | collective-permute-start | bytes 811016 | tf_op jit(solution)/shard_map/ppermute | solution.py:314
  109.8 8.9 %collective-permute-start.17 = (s16[1056,128]{1,0:T(8,128)(2,1)S(1)}, s16[1056,128]{1,0:T(8,128)(2,1)S(1)}, u32[]{:S(2)}, u32[]{:S(2)}) collective-permute-start(s16[1056,128]{1,0:T(8,128)(2,1)S(1)} %get-tuple-element.50), channel_id=1, source_target_pairs={{0,256},{128,384},{256,0},{384,128},{1,257},{129,385},{257,1},{385... | collective-permute-start | bytes 811016 | tf_op jit(solution)/shard_map/ppermute | solution.py:314
  111.7 13.4 %collective-permute-start.18 = (s16[1056,128]{1,0:T(8,128)(2,1)S(1)}, s16[1056,128]{1,0:T(8,128)(2,1)S(1)}, u32[]{:S(2)}, u32[]{:S(2)}) collective-permute-start(s16[1056,128]{1,0:T(8,128)(2,1)S(1)} %get-tuple-element.51), channel_id=1, source_target_pairs={{0,128},{128,256},{256,384},{384,0},{1,129},{129,257},{257,385},{3... | collective-permute-start | bytes 811016 | tf_op jit(solution)/shard_map/ppermute | solution.py:314
  114.2 10.9 %collective-permute-start.19 = (s16[1056,128]{1,0:T(8,128)(2,1)S(1)}, s16[1056,128]{1,0:T(8,128)(2,1)S(1)}, u32[]{:S(2)}, u32[]{:S(2)}) collective-permute-start(s16[1056,128]{1,0:T(8,128)(2,1)S(1)} %get-tuple-element.52), channel_id=1, source_target_pairs={{0,384},{128,0},{256,128},{384,256},{1,385},{129,1},{257,129},{385... | collective-permute-start | bytes 811016 | tf_op jit(solution)/shard_map/ppermute | solution.py:314
Sparse Core Ops, SparseCore 0:
  10.5 54.5 all-gather.2
where the time goes:
time: 136 us; the launch traced here: 134 us
  starting transfers between devices  72.7 us (53%)
  waiting for transfers between devices  23.4 us (17%)
  Pallas kernels  22.7 us (17%)
  between operations  14.4 us (11%)
    ppermute x20, starting transfers between devices, shifted(): lax.ppermute(value, axis, [(i, (i + by) % size) for i in range(size)])  72.7 us
    ppermute x20, waiting for transfers between devices, shifted(): lax.ppermute(value, axis, [(i, (i + by) % size) for i in range(size)])  21.1 us
    pallas_call x5, Pallas kernels, call_products(): pl.pallas_call(kernel, out_shape=out_shape, in_specs=[smem] + [vmem] * (l...  14.7 us
    pallas_call x1, Pallas kernels, prepare(): pl.pallas_call(prepare_kernel, out_shape=[a_send, chunk, chunk], in_specs...  3.12 us
  transfers between devices with their start and end apart: 21, of which 7 were waited for; matrix products, arithmetic and copies ran while one was open for 0% of the time, Pallas kernels for 13%

commit v1 on v0

--- a/solution.py
+++ b/solution.py
@@ -329,7 +329,7 @@
     zero[6], one[2] = up(zero[7]), down(one[1])
     one[6], zero[2] = up(one[7]), down(zero[1])
     zero[5], one[3] = up(zero[6]), down(one[2])
-    (zero[2],) = hold(zero[2])
+    one[6], zero[2] = hold(one[6], zero[2])
     zero[3] = down(zero[2])
     sums = early(zero, one)
     zero[5], *sums = lax.optimization_barrier((zero[5], *sums))

time: 136 us -> 137 us (level)
  waiting for transfers between devices: 23.4 us -> 26.2 us
    ppermute x20, waiting for transfers between devices: 21.1 us -> 23.8 us  [shifted(): lax.ppermute(value, axis, [(i, (i + by) % size) for i in range(size)])]
  transfers between devices with their start and end apart: 21 -> 21, of which waited for: 7 -> 8; matrix products, arithmetic and copies ran while one was open for 0% -> 0% of each run, Pallas kernels for 13% -> 13%
where the time goes in v1:
time: 137 us; the launch traced here: 136 us
  starting transfers between devices  72.6 us (53%)
  waiting for transfers between devices  26.2 us (19%)
  Pallas kernels  22.8 us (17%)
  between operations  14.4 us (11%)
    ppermute x20, starting transfers between devices, shifted(): lax.ppermute(value, axis, [(i, (i + by) % size) for i in range(size)])  72.6 us
    ppermute x20, waiting for transfers between devices, shifted(): lax.ppermute(value, axis, [(i, (i + by) % size) for i in range(size)])  23.8 us
    pallas_call x5, Pallas kernels, call_products(): pl.pallas_call(kernel, out_shape=out_shape, in_specs=[smem] + [vmem] * (l...  14.8 us
    pallas_call x1, Pallas kernels, prepare(): pl.pallas_call(prepare_kernel, out_shape=[a_send, chunk, chunk], in_specs...  3.12 us
  transfers between devices with their start and end apart: 21, of which 8 were waited for; matrix products, arithmetic and copies ran while one was open for 0% of the time, Pallas kernels for 13%

profile of v1, /device:TPU:1, one launch (start us, length us, event | category | flops | bytes accessed | tf_op | source)
XLA Modules:
  0.0 136.0 jit_solution(1226627342506559016)
XLA Ops:
  7.2 3.1 %prepare.1 = (bf16[1552,128]{1,0:T(8,128)(2,1)}, bf16[16,128,128]{2,1,0:T(8,128)(2,1)}, bf16[16,128,128]{2,1,0:T(8,128)(2,1)}) custom-call(bf16[1536,128]{1,0:T(8,128)(2,1)} %bitcast.16, s32[12]{0:T(128)} %bitcast.18, s32[12]{0:T(128)} %bitcast.19, s32[1,1,1]{2,1,0:T(1,128)S(6)} %copy.7.live_ref, bf16[16,2,128,128]{3,2,1,0:T(8,128)(2,1)} %bitcast.15, ...), custom_call_target="tpu_custom_call" | custom-call | tf_op jit(solution)/shard_map/prepare/pallas_call | solution.py:289
  10.3 0.0 all-gather.3.cloned.1.call-update
  10.3 4.9 %collective-permute-start.4 = (bf16[16,128,128]{2,1,0:T(8,128)(2,1)}, bf16[16,128,128]{2,1,0:T(8,128)(2,1)S(1)}, u32[]{:S(2)}, u32[]{:S(2)}) collective-permute-start(bf16[16,128,128]{2,1,0:T(8,128)(2,1)} %get-tuple-element.31.refs_4_), channel_id=1, source_target_pairs={{0,16},{16,32},{32,48},{48,64},{64,80},{80,96},{96,112},{112,0},{1... | collective-permute-start | bytes 1572872 | tf_op jit(solution)/shard_map/ppermute | solution.py:314
  15.2 8.6 %collective-permute-start.7 = (bf16[16,128,128]{2,1,0:T(8,128)(2,1)}, bf16[16,128,128]{2,1,0:T(8,128)(2,1)S(1)}, u32[]{:S(2)}, u32[]{:S(2)}) collective-permute-start(bf16[16,128,128]{2,1,0:T(8,128)(2,1)} %get-tuple-element.30.refs_5_), channel_id=1, source_target_pairs={{0,112},{16,0},{32,16},{48,32},{64,48},{80,64},{96,80},{112,96},{1... | collective-permute-start | bytes 1572872 | tf_op jit(solution)/shard_map/ppermute | solution.py:314
  23.8 1.9 %collective-permute-start = (bf16[16,128,128]{2,1,0:T(8,128)(2,1)}, bf16[16,128,128]{2,1,0:T(8,128)(2,1)}, u32[]{:S(2)}, u32[]{:S(2)}) collective-permute-start(bf16[16,128,128]{2,1,0:T(8,128)(2,1)} %get-tuple-element.30.refs_5_), channel_id=1, source_target_pairs={{0,16},{16,32},{32,48},{48,64},{64,80},{80,96},{96,112},{112,0},{1... | collective-permute-start | bytes 1572872 | tf_op jit(solution)/shard_map/ppermute | solution.py:314
  25.7 4.6 %collective-permute-start.2 = (bf16[16,128,128]{2,1,0:T(8,128)(2,1)}, bf16[16,128,128]{2,1,0:T(8,128)(2,1)}, u32[]{:S(2)}, u32[]{:S(2)}) collective-permute-start(bf16[16,128,128]{2,1,0:T(8,128)(2,1)} %get-tuple-element.31.refs_4_), channel_id=1, source_target_pairs={{0,112},{16,0},{32,16},{48,32},{64,48},{80,64},{96,80},{112,96},{1... | collective-permute-start | bytes 1572872 | tf_op jit(solution)/shard_map/ppermute | solution.py:314
  30.3 3.4 %collective-permute-done.4.refs_0_ = bf16[16,128,128]{2,1,0:T(8,128)(2,1)S(1)} collective-permute-done((bf16[16,128,128]{2,1,0:T(8,128)(2,1)}, bf16[16,128,128]{2,1,0:T(8,128)(2,1)S(1)}, u32[]{:S(2)}, u32[]{:S(2)}) %collective-permute-start.4) | collective-permute-done | bytes 524320 | tf_op jit(solution)/shard_map/ppermute | solution.py:314
  33.7 1.9 %collective-permute-start.5 = (bf16[16,128,128]{2,1,0:T(8,128)(2,1)S(1)}, bf16[16,128,128]{2,1,0:T(8,128)(2,1)S(1)}, u32[]{:S(2)}, u32[]{:S(2)}) collective-permute-start(bf16[16,128,128]{2,1,0:T(8,128)(2,1)S(1)} %collective-permute-done.4.refs_0_), channel_id=1, source_target_pairs={{0,16},{16,32},{32,48},{48,64},{64,80},{80,96},{96,112},{112,0},{1... | collective-permute-start | bytes 1572872 | tf_op jit(solution)/shard_map/ppermute | solution.py:314
  35.6 0.0 collective-permute-done.7.refs_3_
  35.6 4.6 %collective-permute-start.10 = (bf16[16,128,128]{2,1,0:T(8,128)(2,1)S(1)}, bf16[16,128,128]{2,1,0:T(8,128)(2,1)S(1)}, u32[]{:S(2)}, u32[]{:S(2)}) collective-permute-start(bf16[16,128,128]{2,1,0:T(8,128)(2,1)S(1)} %collective-permute-done.7.refs_3_), channel_id=1, source_target_pairs={{0,112},{16,0},{32,16},{48,32},{64,48},{80,64},{96,80},{112,96},{1... | collective-permute-start | bytes 1572872 | tf_op jit(solution)/shard_map/ppermute | solution.py:314
  40.2 4.8 %collective-permute-done.refs_1_ = bf16[16,128,128]{2,1,0:T(8,128)(2,1)} collective-permute-done((bf16[16,128,128]{2,1,0:T(8,128)(2,1)}, bf16[16,128,128]{2,1,0:T(8,128)(2,1)}, u32[]{:S(2)}, u32[]{:S(2)}) %collective-permute-start) | collective-permute-done | bytes 524320 | tf_op jit(solution)/shard_map/ppermute | solution.py:314
  45.0 1.9 %collective-permute-start.1 = (bf16[16,128,128]{2,1,0:T(8,128)(2,1)}, bf16[16,128,128]{2,1,0:T(8,128)(2,1)S(1)}, u32[]{:S(2)}, u32[]{:S(2)}) collective-permute-start(bf16[16,128,128]{2,1,0:T(8,128)(2,1)} %collective-permute-done.refs_1_), channel_id=1, source_target_pairs={{0,16},{16,32},{32,48},{48,64},{64,80},{80,96},{96,112},{112,0},{1... | collective-permute-start | bytes 1572872 | tf_op jit(solution)/shard_map/ppermute | solution.py:314
  46.9 0.0 collective-permute-done.2.refs_2_
  47.0 4.6 %collective-permute-start.3 = (bf16[16,128,128]{2,1,0:T(8,128)(2,1)}, bf16[16,128,128]{2,1,0:T(8,128)(2,1)}, u32[]{:S(2)}, u32[]{:S(2)}) collective-permute-start(bf16[16,128,128]{2,1,0:T(8,128)(2,1)} %collective-permute-done.2.refs_2_), channel_id=1, source_target_pairs={{0,112},{16,0},{32,16},{48,32},{64,48},{80,64},{96,80},{112,96},{1... | collective-permute-start | bytes 1572872 | tf_op jit(solution)/shard_map/ppermute | solution.py:314
  51.5 4.7 %collective-permute-done.5.refs_0_ = bf16[16,128,128]{2,1,0:T(8,128)(2,1)S(1)} collective-permute-done((bf16[16,128,128]{2,1,0:T(8,128)(2,1)S(1)}, bf16[16,128,128]{2,1,0:T(8,128)(2,1)S(1)}, u32[]{:S(2)}, u32[]{:S(2)}) %collective-permute-start.5) | collective-permute-done | bytes 524320 | tf_op jit(solution)/shard_map/ppermute | solution.py:314
  56.3 1.9 %collective-permute-start.6 = (bf16[16,128,128]{2,1,0:T(8,128)(2,1)S(1)}, bf16[16,128,128]{2,1,0:T(8,128)(2,1)}, u32[]{:S(2)}, u32[]{:S(2)}) collective-permute-start(bf16[16,128,128]{2,1,0:T(8,128)(2,1)S(1)} %collective-permute-done.5.refs_0_), channel_id=1, source_target_pairs={{0,16},{16,32},{32,48},{48,64},{64,80},{80,96},{96,112},{112,0},{1... | collective-permute-start | bytes 1572872 | tf_op jit(solution)/shard_map/ppermute | solution.py:314
  58.2 0.0 collective-permute-done.10.refs_3_
  58.2 4.6 %collective-permute-start.11 = (bf16[16,128,128]{2,1,0:T(8,128)(2,1)S(1)}, bf16[16,128,128]{2,1,0:T(8,128)(2,1)S(1)}, u32[]{:S(2)}, u32[]{:S(2)}) collective-permute-start(bf16[16,128,128]{2,1,0:T(8,128)(2,1)S(1)} %collective-permute-done.10.refs_3_), channel_id=1, source_target_pairs={{0,112},{16,0},{32,16},{48,32},{64,48},{80,64},{96,80},{112,96},{1... | collective-permute-start | bytes 1572872 | tf_op jit(solution)/shard_map/ppermute | solution.py:314
  62.8 2.3 %all-gather.3.cloned.1.call-done = bf16[24832,128]{1,0:T(8,128)(2,1)} async-done(((bf16[1552,128]{1,0:T(8,128)(2,1)}), bf16[24832,128]{1,0:T(8,128)(2,1)}) %all-gather.3.cloned.1.call-update) | async-done | bytes 6357008 | tf_op jit(solution)/shard_map/all_gather | solution.py:351
  65.1 2.4 %positions.1.place_ref = s32[16,128]{1,0:T(8,128)S(1)} custom-call(bf16[16,1552,128]{2,1,0:T(8,128)(2,1)} %bitcast.9), custom_call_target="tpu_custom_call" | custom-call | flops 5000000000 | bytes 1048576 | tf_op jit(solution)/shard_map/positions/pallas_call | solution.py:142
  67.5 0.0 copy-start.1
  67.5 0.0 collective-permute-done.1.refs_1_
  67.5 0.8 collective-permute-done.3.refs_2_
  68.4 5.3 %collective-permute-start.9 = (bf16[16,128,128]{2,1,0:T(8,128)(2,1)}, bf16[16,128,128]{2,1,0:T(8,128)(2,1)S(1)}, u32[]{:S(2)}, u32[]{:S(2)}) collective-permute-start(bf16[16,128,128]{2,1,0:T(8,128)(2,1)} %collective-permute-done.3.refs_2_), channel_id=1, source_target_pairs={{0,112},{16,0},{32,16},{48,32},{64,48},{80,64},{96,80},{112,96},{1... | collective-permute-start | bytes 1572872 | tf_op jit(solution)/shard_map/ppermute | solution.py:314
  73.7 3.0 %open_sums.3 = (f32[33,128,128]{2,1,0:T(8,128)S(1)}, f32[33,128,128]{2,1,0:T(8,128)S(1)}) custom-call(s32[16,128]{1,0:T(8,128)S(1)} %positions.1.place_ref, bf16[16,1552,128]{2,1,0:T(8,128)(2,1)S(1)} %bitcast.10, bf16[16,128,128]{2,1,0:T(8,128)(2,1)S(1)} %collective-permute-done.4.refs_0_, bf16[16,128,128]{2,1,0:T(8,128)(2,1)} %collective-permute-done.refs_1_, ...), custom_call_target="tpu_custom_call" | custom-call | flops 5000000000 | bytes 1048576 | tf_op jit(solution)/shard_map/open_sums/pallas_call | solution.py:161
  76.7 2.0 %collective-permute-done.6.refs_6_ = bf16[16,128,128]{2,1,0:T(8,128)(2,1)} collective-permute-done((bf16[16,128,128]{2,1,0:T(8,128)(2,1)S(1)}, bf16[16,128,128]{2,1,0:T(8,128)(2,1)}, u32[]{:S(2)}, u32[]{:S(2)}) %collective-permute-start.6) | collective-permute-done | bytes 524320 | tf_op jit(solution)/shard_map/ppermute | solution.py:314
  78.7 1.9 %collective-permute-start.8 = (bf16[16,128,128]{2,1,0:T(8,128)(2,1)}, bf16[16,128,128]{2,1,0:T(8,128)(2,1)S(1)}, u32[]{:S(2)}, u32[]{:S(2)}) collective-permute-start(bf16[16,128,128]{2,1,0:T(8,128)(2,1)} %collective-permute-done.6.refs_6_), channel_id=1, source_target_pairs={{0,16},{16,32},{32,48},{48,64},{64,80},{80,96},{96,112},{112,0},{1... | collective-permute-start | bytes 1572872 | tf_op jit(solution)/shard_map/ppermute | solution.py:314
  80.7 0.0 collective-permute-done.11.refs_7_
  80.7 4.9 %open_sums.4 = (f32[33,128,128]{2,1,0:T(8,128)S(1)}, f32[33,128,128]{2,1,0:T(8,128)S(1)}) custom-call(s32[16,128]{1,0:T(8,128)S(1)} %positions.1.place_ref, bf16[16,1552,128]{2,1,0:T(8,128)(2,1)S(1)} %bitcast.11, bf16[16,128,128]{2,1,0:T(8,128)(2,1)S(1)} %collective-permute-done.5.refs_0_, bf16[16,128,128]{2,1,0:T(8,128)(2,1)S(1)} %collective-permute-done.1.refs_1_, ...), custom_call_target="tpu_custom_call" | custom-call | flops 5000000000 | bytes 1048576 | tf_op jit(solution)/shard_map/open_sums/pallas_call | solution.py:161
  85.6 4.6 %collective-permute-start.15 = (bf16[16,128,128]{2,1,0:T(8,128)(2,1)S(1)}, bf16[16,128,128]{2,1,0:T(8,128)(2,1)S(1)}, u32[]{:S(2)}, u32[]{:S(2)}) collective-permute-start(bf16[16,128,128]{2,1,0:T(8,128)(2,1)S(1)} %collective-permute-done.11.refs_7_), channel_id=1, source_target_pairs={{0,112},{16,0},{32,16},{48,32},{64,48},{80,64},{96,80},{112,96},{1... | collective-permute-start | bytes 1572872 | tf_op jit(solution)/shard_map/ppermute | solution.py:314
  90.2 1.9 %collective-permute-start.16 = (bf16[16,128,128]{2,1,0:T(8,128)(2,1)S(1)}, bf16[16,128,128]{2,1,0:T(8,128)(2,1)S(1)}, u32[]{:S(2)}, u32[]{:S(2)}) collective-permute-start(bf16[16,128,128]{2,1,0:T(8,128)(2,1)S(1)} %collective-permute-done.1.refs_1_), channel_id=1, source_target_pairs={{0,16},{16,32},{32,48},{48,64},{64,80},{80,96},{96,112},{112,0},{1... | collective-permute-start | bytes 1572872 | tf_op jit(solution)/shard_map/ppermute | solution.py:314
  92.1 0.0 collective-permute-done.9.refs_0_
  92.1 1.4 %open_sums.5.refs_1_ = f32[33,128,128]{2,1,0:T(8,128)S(1)} custom-call(s32[16,128]{1,0:T(8,128)S(1)} %positions.1.place_ref, bf16[16,1552,128]{2,1,0:T(8,128)(2,1)S(1)} %bitcast.12, bf16[16,128,128]{2,1,0:T(8,128)(2,1)S(1)} %collective-permute-done.9.refs_0_, f32[33,128,128]{2,1,0:T(8,128)S(1)} %get-tuple-element.43.refs_1_), custom_call_target="tpu_custom_call" | custom-call | flops 5000000000 | bytes 1048576 | tf_op jit(solution)/shard_map/open_sums/pallas_call | solution.py:161
  93.6 0.6 collective-permute-done.8.refs_0_
  94.2 2.4 %close_sums.2 = (f32[32,32,128]{2,1,0:T(8,128)S(1)}, s16[1056,128]{1,0:T(8,128)(2,1)S(1)}, s16[1056,128]{1,0:T(8,128)(2,1)S(1)}, s16[1056,128]{1,0:T(8,128)(2,1)S(1)}) custom-call(s32[16,128]{1,0:T(8,128)S(1)} %positions.1.place_ref, bf16[16,1552,128]{2,1,0:T(8,128)(2,1)S(1)} %bitcast.13, bf16[16,128,128]{2,1,0:T(8,128)(2,1)S(1)} %collective-permute-done.8.refs_0_, ...), custom_call_target="tpu_custom_call" | custom-call | flops 20000000000 | bytes 1048576 | tf_op jit(solution)/shard_map/close_sums/pallas_call | solution.py:161
  96.7 4.7 %collective-permute-start.12 = (s16[1056,128]{1,0:T(8,128)(2,1)S(1)}, s16[1056,128]{1,0:T(8,128)(2,1)S(1)}, u32[]{:S(2)}, u32[]{:S(2)}) collective-permute-start(s16[1056,128]{1,0:T(8,128)(2,1)S(1)} %get-tuple-element.45), channel_id=1, source_target_pairs={{0,256},{128,384},{256,0},{384,128},{1,257},{129,385},{257,1},{385... | collective-permute-start | bytes 811016 | tf_op jit(solution)/shard_map/ppermute | solution.py:314
  101.3 2.2 %collective-permute-start.13 = (s16[1056,128]{1,0:T(8,128)(2,1)S(1)}, s16[1056,128]{1,0:T(8,128)(2,1)S(1)}, u32[]{:S(2)}, u32[]{:S(2)}) collective-permute-start(s16[1056,128]{1,0:T(8,128)(2,1)S(1)} %get-tuple-element.46), channel_id=1, source_target_pairs={{0,128},{128,256},{256,384},{384,0},{1,129},{129,257},{257,385},{3... | collective-permute-start | bytes 811016 | tf_op jit(solution)/shard_map/ppermute | solution.py:314
  103.5 4.3 %collective-permute-start.14 = (s16[1056,128]{1,0:T(8,128)(2,1)S(1)}, s16[1056,128]{1,0:T(8,128)(2,1)S(1)}, u32[]{:S(2)}, u32[]{:S(2)}) collective-permute-start(s16[1056,128]{1,0:T(8,128)(2,1)S(1)} %get-tuple-element.47), channel_id=1, source_target_pairs={{0,384},{128,0},{256,128},{384,256},{1,385},{129,1},{257,129},{385... | collective-permute-start | bytes 811016 | tf_op jit(solution)/shard_map/ppermute | solution.py:314
  107.8 3.0 %close_sums.3 = (f32[32,32,128]{2,1,0:T(8,128)S(1)}, s16[1056,128]{1,0:T(8,128)(2,1)S(1)}, s16[1056,128]{1,0:T(8,128)(2,1)S(1)}, s16[1056,128]{1,0:T(8,128)(2,1)S(1)}) custom-call(s32[16,128]{1,0:T(8,128)S(1)} %positions.1.place_ref, bf16[16,1552,128]{2,1,0:T(8,128)(2,1)S(1)} %bitcast.14, bf16[16,128,128]{2,1,0:T(8,128)(2,1)S(1)} %collective-permute-done.15.refs_0_, ...), custom_call_target="tpu_custom_call" | custom-call | flops 99999997952 | bytes 1048576 | tf_op jit(solution)/shard_map/close_sums/pallas_call | solution.py:161
  110.8 1.9 %collective-permute-start.17 = (s16[1056,128]{1,0:T(8,128)(2,1)S(1)}, s16[1056,128]{1,0:T(8,128)(2,1)S(1)}, u32[]{:S(2)}, u32[]{:S(2)}) collective-permute-start(s16[1056,128]{1,0:T(8,128)(2,1)S(1)} %get-tuple-element.52), channel_id=1, source_target_pairs={{0,256},{128,384},{256,0},{384,128},{1,257},{129,385},{257,1},{385... | collective-permute-start | bytes 811016 | tf_op jit(solution)/shard_map/ppermute | solution.py:314
  112.8 2.5 %collective-permute-start.18 = (s16[1056,128]{1,0:T(8,128)(2,1)S(1)}, s16[1056,128]{1,0:T(8,128)(2,1)S(1)}, u32[]{:S(2)}, u32[]{:S(2)}) collective-permute-start(s16[1056,128]{1,0:T(8,128)(2,1)S(1)} %get-tuple-element.53), channel_id=1, source_target_pairs={{0,128},{128,256},{256,384},{384,0},{1,129},{129,257},{257,385},{3... | collective-permute-start | bytes 811016 | tf_op jit(solution)/shard_map/ppermute | solution.py:314
  115.3 4.0 %collective-permute-start.19 = (s16[1056,128]{1,0:T(8,128)(2,1)S(1)}, s16[1056,128]{1,0:T(8,128)(2,1)S(1)}, u32[]{:S(2)}, u32[]{:S(2)}) collective-permute-start(s16[1056,128]{1,0:T(8,128)(2,1)S(1)} %get-tuple-element.54), channel_id=1, source_target_pairs={{0,384},{128,0},{256,128},{384,256},{1,385},{129,1},{257,129},{385... | collective-permute-start | bytes 811016 | tf_op jit(solution)/shard_map/ppermute | solution.py:314
  119.3 0.0 collective-permute-done.13.refs_1_
  119.3 0.0 collective-permute-done.14.refs_2_
  119.3 0.4 first_combine.1.first_ref
  119.7 7.3 %collective-permute-done.18.refs_1_ = s16[1056,128]{1,0:T(8,128)(2,1)S(1)} collective-permute-done((s16[1056,128]{1,0:T(8,128)(2,1)S(1)}, s16[1056,128]{1,0:T(8,128)(2,1)S(1)}, u32[]{:S(2)}, u32[]{:S(2)}) %collective-permute-start.18) | collective-permute-done | bytes 270368 | tf_op jit(solution)/shard_map/ppermute | solution.py:314
  127.0 0.0 collective-permute-done.19.refs_2_
  127.1 2.1 %last_combine.1 = f32[2048,128]{1,0:T(8,128)} custom-call(f32[32,32,128]{2,1,0:T(8,128)S(1)} %first_combine.1.first_ref, f32[32,32,128]{2,1,0:T(8,128)S(1)} %get-tuple-element.51.own_ref, s16[1056,128]{1,0:T(8,128)(2,1)S(1)} %collective-permute-done.17.refs_0_, s16[1056,128]{1,0:T(8,128)(2,1)S(1)} %collective-permute-done.18.refs_1_, ...), custom_call_target="tpu_custom_call" | custom-call | flops 1000000000 | bytes 1048576 | tf_op jit(solution)/shard_map/last_combine/pallas_call | solution.py:241
  (10 shorter events, 0.0 us)
Async XLA Ops:
  6.5 58.6 %all-gather.3.cloned.1.call-start = ((), (), s32[]{:S(2)}) async-start(), calls=%async_computation | async-start | bytes 6754304 | tf_op jit(solution)/shard_map/all_gather | solution.py:351
  10.3 23.3 %collective-permute-start.4 = (bf16[16,128,128]{2,1,0:T(8,128)(2,1)}, bf16[16,128,128]{2,1,0:T(8,128)(2,1)S(1)}, u32[]{:S(2)}, u32[]{:S(2)}) collective-permute-start(bf16[16,128,128]{2,1,0:T(8,128)(2,1)} %get-tuple-element.31.refs_4_), channel_id=1, source_target_pairs={{0,16},{16,32},{32,48},{48,64},{64,80},{80,96},{96,112},{112,0},{1... | collective-permute-start | bytes 1572872 | tf_op jit(solution)/shard_map/ppermute | solution.py:314
  15.2 20.4 %collective-permute-start.7 = (bf16[16,128,128]{2,1,0:T(8,128)(2,1)}, bf16[16,128,128]{2,1,0:T(8,128)(2,1)S(1)}, u32[]{:S(2)}, u32[]{:S(2)}) collective-permute-start(bf16[16,128,128]{2,1,0:T(8,128)(2,1)} %get-tuple-element.30.refs_5_), channel_id=1, source_target_pairs={{0,112},{16,0},{32,16},{48,32},{64,48},{80,64},{96,80},{112,96},{1... | collective-permute-start | bytes 1572872 | tf_op jit(solution)/shard_map/ppermute | solution.py:314
  23.8 21.3 %collective-permute-start = (bf16[16,128,128]{2,1,0:T(8,128)(2,1)}, bf16[16,128,128]{2,1,0:T(8,128)(2,1)}, u32[]{:S(2)}, u32[]{:S(2)}) collective-permute-start(bf16[16,128,128]{2,1,0:T(8,128)(2,1)} %get-tuple-element.30.refs_5_), channel_id=1, source_target_pairs={{0,16},{16,32},{32,48},{48,64},{64,80},{80,96},{96,112},{112,0},{1... | collective-permute-start | bytes 1572872 | tf_op jit(solution)/shard_map/ppermute | solution.py:314
  25.7 21.2 %collective-permute-start.2 = (bf16[16,128,128]{2,1,0:T(8,128)(2,1)}, bf16[16,128,128]{2,1,0:T(8,128)(2,1)}, u32[]{:S(2)}, u32[]{:S(2)}) collective-permute-start(bf16[16,128,128]{2,1,0:T(8,128)(2,1)} %get-tuple-element.31.refs_4_), channel_id=1, source_target_pairs={{0,112},{16,0},{32,16},{48,32},{64,48},{80,64},{96,80},{112,96},{1... | collective-permute-start | bytes 1572872 | tf_op jit(solution)/shard_map/ppermute | solution.py:314
  33.7 22.6 %collective-permute-start.5 = (bf16[16,128,128]{2,1,0:T(8,128)(2,1)S(1)}, bf16[16,128,128]{2,1,0:T(8,128)(2,1)S(1)}, u32[]{:S(2)}, u32[]{:S(2)}) collective-permute-start(bf16[16,128,128]{2,1,0:T(8,128)(2,1)S(1)} %collective-permute-done.4.refs_0_), channel_id=1, source_target_pairs={{0,16},{16,32},{32,48},{48,64},{64,80},{80,96},{96,112},{112,0},{1... | collective-permute-start | bytes 1572872 | tf_op jit(solution)/shard_map/ppermute | solution.py:314
  35.6 22.6 %collective-permute-start.10 = (bf16[16,128,128]{2,1,0:T(8,128)(2,1)S(1)}, bf16[16,128,128]{2,1,0:T(8,128)(2,1)S(1)}, u32[]{:S(2)}, u32[]{:S(2)}) collective-permute-start(bf16[16,128,128]{2,1,0:T(8,128)(2,1)S(1)} %collective-permute-done.7.refs_3_), channel_id=1, source_target_pairs={{0,112},{16,0},{32,16},{48,32},{64,48},{80,64},{96,80},{112,96},{1... | collective-permute-start | bytes 1572872 | tf_op jit(solution)/shard_map/ppermute | solution.py:314
  45.0 22.5 %collective-permute-start.1 = (bf16[16,128,128]{2,1,0:T(8,128)(2,1)}, bf16[16,128,128]{2,1,0:T(8,128)(2,1)S(1)}, u32[]{:S(2)}, u32[]{:S(2)}) collective-permute-start(bf16[16,128,128]{2,1,0:T(8,128)(2,1)} %collective-permute-done.refs_1_), channel_id=1, source_target_pairs={{0,16},{16,32},{32,48},{48,64},{64,80},{80,96},{96,112},{112,0},{1... | collective-permute-start | bytes 1572872 | tf_op jit(solution)/shard_map/ppermute | solution.py:314
  47.0 21.4 %collective-permute-start.3 = (bf16[16,128,128]{2,1,0:T(8,128)(2,1)}, bf16[16,128,128]{2,1,0:T(8,128)(2,1)}, u32[]{:S(2)}, u32[]{:S(2)}) collective-permute-start(bf16[16,128,128]{2,1,0:T(8,128)(2,1)} %collective-permute-done.2.refs_2_), channel_id=1, source_target_pairs={{0,112},{16,0},{32,16},{48,32},{64,48},{80,64},{96,80},{112,96},{1... | collective-permute-start | bytes 1572872 | tf_op jit(solution)/shard_map/ppermute | solution.py:314
  56.3 22.5 %collective-permute-start.6 = (bf16[16,128,128]{2,1,0:T(8,128)(2,1)S(1)}, bf16[16,128,128]{2,1,0:T(8,128)(2,1)}, u32[]{:S(2)}, u32[]{:S(2)}) collective-permute-start(bf16[16,128,128]{2,1,0:T(8,128)(2,1)S(1)} %collective-permute-done.5.refs_0_), channel_id=1, source_target_pairs={{0,16},{16,32},{32,48},{48,64},{64,80},{80,96},{96,112},{112,0},{1... | collective-permute-start | bytes 1572872 | tf_op jit(solution)/shard_map/ppermute | solution.py:314
  58.2 22.5 %collective-permute-start.11 = (bf16[16,128,128]{2,1,0:T(8,128)(2,1)S(1)}, bf16[16,128,128]{2,1,0:T(8,128)(2,1)S(1)}, u32[]{:S(2)}, u32[]{:S(2)}) collective-permute-start(bf16[16,128,128]{2,1,0:T(8,128)(2,1)S(1)} %collective-permute-done.10.refs_3_), channel_id=1, source_target_pairs={{0,112},{16,0},{32,16},{48,32},{64,48},{80,64},{96,80},{112,96},{1... | collective-permute-start | bytes 1572872 | tf_op jit(solution)/shard_map/ppermute | solution.py:314
  65.1 8.6 %copy-start = (bf16[24832,128]{1,0:T(8,128)(2,1)S(1)}, bf16[24832,128]{1,0:T(8,128)(2,1)}, u32[]{:S(2)}) copy-start(bf16[24832,128]{1,0:T(8,128)(2,1)} %all-gather.3.cloned.1.call-done) | copy-start | bytes 19070980
  67.5 13.2 %copy-start.1 = (bf16[16,128,128]{2,1,0:T(8,128)(2,1)S(1)}, bf16[16,128,128]{2,1,0:T(8,128)(2,1)}, u32[]{:S(2)}) copy-start(bf16[16,128,128]{2,1,0:T(8,128)(2,1)} %get-tuple-element.31.refs_4_) | copy-start | bytes 1572868
  67.5 13.2 %copy-start.2 = (bf16[16,128,128]{2,1,0:T(8,128)(2,1)S(1)}, bf16[16,128,128]{2,1,0:T(8,128)(2,1)}, u32[]{:S(2)}) copy-start(bf16[16,128,128]{2,1,0:T(8,128)(2,1)} %get-tuple-element.30.refs_5_) | copy-start | bytes 1572868
  68.4 23.8 %collective-permute-start.9 = (bf16[16,128,128]{2,1,0:T(8,128)(2,1)}, bf16[16,128,128]{2,1,0:T(8,128)(2,1)S(1)}, u32[]{:S(2)}, u32[]{:S(2)}) collective-permute-start(bf16[16,128,128]{2,1,0:T(8,128)(2,1)} %collective-permute-done.3.refs_2_), channel_id=1, source_target_pairs={{0,112},{16,0},{32,16},{48,32},{64,48},{80,64},{96,80},{112,96},{1... | collective-permute-start | bytes 1572872 | tf_op jit(solution)/shard_map/ppermute | solution.py:314
  78.7 15.5 %collective-permute-start.8 = (bf16[16,128,128]{2,1,0:T(8,128)(2,1)}, bf16[16,128,128]{2,1,0:T(8,128)(2,1)S(1)}, u32[]{:S(2)}, u32[]{:S(2)}) collective-permute-start(bf16[16,128,128]{2,1,0:T(8,128)(2,1)} %collective-permute-done.6.refs_6_), channel_id=1, source_target_pairs={{0,16},{16,32},{32,48},{48,64},{64,80},{80,96},{96,112},{112,0},{1... | collective-permute-start | bytes 1572872 | tf_op jit(solution)/shard_map/ppermute | solution.py:314
  85.6 22.2 %collective-permute-start.15 = (bf16[16,128,128]{2,1,0:T(8,128)(2,1)S(1)}, bf16[16,128,128]{2,1,0:T(8,128)(2,1)S(1)}, u32[]{:S(2)}, u32[]{:S(2)}) collective-permute-start(bf16[16,128,128]{2,1,0:T(8,128)(2,1)S(1)} %collective-permute-done.11.refs_7_), channel_id=1, source_target_pairs={{0,112},{16,0},{32,16},{48,32},{64,48},{80,64},{96,80},{112,96},{1... | collective-permute-start | bytes 1572872 | tf_op jit(solution)/shard_map/ppermute | solution.py:314
  90.2 17.6 %collective-permute-start.16 = (bf16[16,128,128]{2,1,0:T(8,128)(2,1)S(1)}, bf16[16,128,128]{2,1,0:T(8,128)(2,1)S(1)}, u32[]{:S(2)}, u32[]{:S(2)}) collective-permute-start(bf16[16,128,128]{2,1,0:T(8,128)(2,1)S(1)} %collective-permute-done.1.refs_1_), channel_id=1, source_target_pairs={{0,16},{16,32},{32,48},{48,64},{64,80},{80,96},{96,112},{112,0},{1... | collective-permute-start | bytes 1572872 | tf_op jit(solution)/shard_map/ppermute | solution.py:314
  96.7 18.6 %collective-permute-start.12 = (s16[1056,128]{1,0:T(8,128)(2,1)S(1)}, s16[1056,128]{1,0:T(8,128)(2,1)S(1)}, u32[]{:S(2)}, u32[]{:S(2)}) collective-permute-start(s16[1056,128]{1,0:T(8,128)(2,1)S(1)} %get-tuple-element.45), channel_id=1, source_target_pairs={{0,256},{128,384},{256,0},{384,128},{1,257},{129,385},{257,1},{385... | collective-permute-start | bytes 811016 | tf_op jit(solution)/shard_map/ppermute | solution.py:314
  101.3 18.0 %collective-permute-start.13 = (s16[1056,128]{1,0:T(8,128)(2,1)S(1)}, s16[1056,128]{1,0:T(8,128)(2,1)S(1)}, u32[]{:S(2)}, u32[]{:S(2)}) collective-permute-start(s16[1056,128]{1,0:T(8,128)(2,1)S(1)} %get-tuple-element.46), channel_id=1, source_target_pairs={{0,128},{128,256},{256,384},{384,0},{1,129},{129,257},{257,385},{3... | collective-permute-start | bytes 811016 | tf_op jit(solution)/shard_map/ppermute | solution.py:314
  103.5 15.7 %collective-permute-start.14 = (s16[1056,128]{1,0:T(8,128)(2,1)S(1)}, s16[1056,128]{1,0:T(8,128)(2,1)S(1)}, u32[]{:S(2)}, u32[]{:S(2)}) collective-permute-start(s16[1056,128]{1,0:T(8,128)(2,1)S(1)} %get-tuple-element.47), channel_id=1, source_target_pairs={{0,384},{128,0},{256,128},{384,256},{1,385},{129,1},{257,129},{385... | collective-permute-start | bytes 811016 | tf_op jit(solution)/shard_map/ppermute | solution.py:314
  110.8 8.9 %collective-permute-start.17 = (s16[1056,128]{1,0:T(8,128)(2,1)S(1)}, s16[1056,128]{1,0:T(8,128)(2,1)S(1)}, u32[]{:S(2)}, u32[]{:S(2)}) collective-permute-start(s16[1056,128]{1,0:T(8,128)(2,1)S(1)} %get-tuple-element.52), channel_id=1, source_target_pairs={{0,256},{128,384},{256,0},{384,128},{1,257},{129,385},{257,1},{385... | collective-permute-start | bytes 811016 | tf_op jit(solution)/shard_map/ppermute | solution.py:314
  112.8 14.3 %collective-permute-start.18 = (s16[1056,128]{1,0:T(8,128)(2,1)S(1)}, s16[1056,128]{1,0:T(8,128)(2,1)S(1)}, u32[]{:S(2)}, u32[]{:S(2)}) collective-permute-start(s16[1056,128]{1,0:T(8,128)(2,1)S(1)} %get-tuple-element.53), channel_id=1, source_target_pairs={{0,128},{128,256},{256,384},{384,0},{1,129},{129,257},{257,385},{3... | collective-permute-start | bytes 811016 | tf_op jit(solution)/shard_map/ppermute | solution.py:314
  115.3 11.8 %collective-permute-start.19 = (s16[1056,128]{1,0:T(8,128)(2,1)S(1)}, s16[1056,128]{1,0:T(8,128)(2,1)S(1)}, u32[]{:S(2)}, u32[]{:S(2)}) collective-permute-start(s16[1056,128]{1,0:T(8,128)(2,1)S(1)} %get-tuple-element.54), channel_id=1, source_target_pairs={{0,384},{128,0},{256,128},{384,256},{1,385},{129,1},{257,129},{385... | collective-permute-start | bytes 811016 | tf_op jit(solution)/shard_map/ppermute | solution.py:314
Sparse Core Ops, SparseCore 0:
  10.5 54.5 all-gather.2

commit v2 on v1

--- a/solution.py
+++ b/solution.py
@@ -329,9 +329,9 @@
     zero[6], one[2] = up(zero[7]), down(one[1])
     one[6], zero[2] = up(one[7]), down(zero[1])
     zero[5], one[3] = up(zero[6]), down(one[2])
-    one[6], zero[2] = hold(one[6], zero[2])
+    zero[2], *sums = hold(zero, one)
     zero[3] = down(zero[2])
-    sums = early(zero, one)
+    sums = early(zero, one, sums)
     zero[5], *sums = lax.optimization_barrier((zero[5], *sums))
     zero[4] = up(zero[5])
     sums = middle(zero, one, sums)
@@ -351,15 +351,15 @@
     a_all = lax.all_gather(a_send, "col", axis=0)
     where = [positions(a_all), a_all]
 
-    def hold(*behind):
-        *behind, where[0] = lax.optimization_barrier((*behind, where[0]))
-        return behind
-
-    def early(zero, one):
-        return open_sums(where, (zero, one), (7, 1), ((), ()))
+    def hold(zero, one):
+        sums = open_sums(where, (zero, one), (7, 1), ((), ()))
+        return lax.optimization_barrier((zero[2], *sums))
+
+    def early(zero, one, sums):
+        return open_sums(where, (zero, one), (6, 2), ((), ()), sums)
 
     def middle(zero, one, sums):
-        return open_sums(where, (zero, one), (6, 2, 0), ((5,), (3,)), sums)
+        return open_sums(where, (zero, one), (0,), ((5,), (3,)), sums)
 
     zero, one, sums = around(b_zero, b_one, hold, early, middle)
     before = open_sums(where, (zero,), (), ((3,),), sums[:1])

time: 137 us -> 138 us (level)
    pallas_call x5 -> x6, Pallas kernels: 14.8 us -> 15.6 us  [call_products(): pl.pallas_call(kernel, out_shape=out_shape, in_specs=[smem] + [vmem] * (l...]
  transfers between devices with their start and end apart: 21 -> 21, of which waited for: 8 -> 6; matrix products, arithmetic and copies ran while one was open for 0% -> 0% of each run, Pallas kernels for 13% -> 13%
where the time goes in v2:
time: 138 us; the launch traced here: 137 us
  starting transfers between devices  72.9 us (53%)
  waiting for transfers between devices  25 us (18%)
  Pallas kernels  23.7 us (17%)
  between operations  14.4 us (10%)
    ppermute x20, starting transfers between devices, shifted(): lax.ppermute(value, axis, [(i, (i + by) % size) for i in range(size)])  72.9 us
    ppermute x20, waiting for transfers between devices, shifted(): lax.ppermute(value, axis, [(i, (i + by) % size) for i in range(size)])  22.7 us
    pallas_call x6, Pallas kernels, call_products(): pl.pallas_call(kernel, out_shape=out_shape, in_specs=[smem] + [vmem] * (l...  15.6 us
    pallas_call x1, Pallas kernels, prepare(): pl.pallas_call(prepare_kernel, out_shape=[a_send, chunk, chunk], in_specs...  3.11 us
  transfers between devices with their start and end apart: 21, of which 6 were waited for; matrix products, arithmetic and copies ran while one was open for 0% of the time, Pallas kernels for 13%

profile of v2, /device:TPU:1, one launch (start us, length us, event | category | flops | bytes accessed | tf_op | source)
XLA Modules:
  0.0 137.3 jit_solution(116156809809252708)
XLA Ops:
  7.2 3.1 %prepare.1 = (bf16[1552,128]{1,0:T(8,128)(2,1)}, bf16[16,128,128]{2,1,0:T(8,128)(2,1)}, bf16[16,128,128]{2,1,0:T(8,128)(2,1)}) custom-call(bf16[1536,128]{1,0:T(8,128)(2,1)} %bitcast.17, s32[12]{0:T(128)} %bitcast.19, s32[12]{0:T(128)} %bitcast.20, s32[1,1,1]{2,1,0:T(1,128)S(6)} %copy.7.live_ref, bf16[16,2,128,128]{3,2,1,0:T(8,128)(2,1)} %bitcast.16, ...), custom_call_target="tpu_custom_call" | custom-call | tf_op jit(solution)/shard_map/prepare/pallas_call | solution.py:289
  10.3 0.0 all-gather.3.cloned.1.call-update
  10.3 4.9 %collective-permute-start = (bf16[16,128,128]{2,1,0:T(8,128)(2,1)}, bf16[16,128,128]{2,1,0:T(8,128)(2,1)S(1)}, u32[]{:S(2)}, u32[]{:S(2)}) collective-permute-start(bf16[16,128,128]{2,1,0:T(8,128)(2,1)} %get-tuple-element.33.refs_0_), channel_id=1, source_target_pairs={{0,16},{16,32},{32,48},{48,64},{64,80},{80,96},{96,112},{112,0},{1... | collective-permute-start | bytes 1572872 | tf_op jit(solution)/shard_map/ppermute | solution.py:314
  15.2 8.6 %collective-permute-start.7 = (bf16[16,128,128]{2,1,0:T(8,128)(2,1)}, bf16[16,128,128]{2,1,0:T(8,128)(2,1)S(1)}, u32[]{:S(2)}, u32[]{:S(2)}) collective-permute-start(bf16[16,128,128]{2,1,0:T(8,128)(2,1)} %get-tuple-element.34.refs_1_), channel_id=1, source_target_pairs={{0,112},{16,0},{32,16},{48,32},{64,48},{80,64},{96,80},{112,96},{1... | collective-permute-start | bytes 1572872 | tf_op jit(solution)/shard_map/ppermute | solution.py:314
  23.8 3.4 %collective-permute-start.5 = (bf16[16,128,128]{2,1,0:T(8,128)(2,1)}, bf16[16,128,128]{2,1,0:T(8,128)(2,1)}, u32[]{:S(2)}, u32[]{:S(2)}) collective-permute-start(bf16[16,128,128]{2,1,0:T(8,128)(2,1)} %get-tuple-element.33.refs_0_), channel_id=1, source_target_pairs={{0,112},{16,0},{32,16},{48,32},{64,48},{80,64},{96,80},{112,96},{1... | collective-permute-start | bytes 1572872 | tf_op jit(solution)/shard_map/ppermute | solution.py:314
  27.1 1.9 %collective-permute-start.3 = (bf16[16,128,128]{2,1,0:T(8,128)(2,1)}, bf16[16,128,128]{2,1,0:T(8,128)(2,1)}, u32[]{:S(2)}, u32[]{:S(2)}) collective-permute-start(bf16[16,128,128]{2,1,0:T(8,128)(2,1)} %get-tuple-element.34.refs_1_), channel_id=1, source_target_pairs={{0,16},{16,32},{32,48},{48,64},{64,80},{80,96},{96,112},{112,0},{1... | collective-permute-start | bytes 1572872 | tf_op jit(solution)/shard_map/ppermute | solution.py:314
  29.1 4.6 %collective-permute-done.refs_0_ = bf16[16,128,128]{2,1,0:T(8,128)(2,1)S(1)} collective-permute-done((bf16[16,128,128]{2,1,0:T(8,128)(2,1)}, bf16[16,128,128]{2,1,0:T(8,128)(2,1)S(1)}, u32[]{:S(2)}, u32[]{:S(2)}) %collective-permute-start) | collective-permute-done | bytes 524320 | tf_op jit(solution)/shard_map/ppermute | solution.py:314
  33.7 1.9 %collective-permute-start.1 = (bf16[16,128,128]{2,1,0:T(8,128)(2,1)S(1)}, bf16[16,128,128]{2,1,0:T(8,128)(2,1)}, u32[]{:S(2)}, u32[]{:S(2)}) collective-permute-start(bf16[16,128,128]{2,1,0:T(8,128)(2,1)S(1)} %collective-permute-done.refs_0_), channel_id=1, source_target_pairs={{0,16},{16,32},{32,48},{48,64},{64,80},{80,96},{96,112},{112,0},{1... | collective-permute-start | bytes 1572872 | tf_op jit(solution)/shard_map/ppermute | solution.py:314
  35.6 4.6 %collective-permute-start.8 = (bf16[16,128,128]{2,1,0:T(8,128)(2,1)S(1)}, bf16[16,128,128]{2,1,0:T(8,128)(2,1)S(1)}, u32[]{:S(2)}, u32[]{:S(2)}) collective-permute-start(bf16[16,128,128]{2,1,0:T(8,128)(2,1)S(1)} %collective-permute-done.7.refs_3_), channel_id=1, source_target_pairs={{0,112},{16,0},{32,16},{48,32},{64,48},{80,64},{96,80},{112,96},{1... | collective-permute-start | bytes 1572872 | tf_op jit(solution)/shard_map/ppermute | solution.py:314
  40.2 0.8 copy-done.3
  41.0 4.9 %collective-permute-done.5.refs_2_ = bf16[16,128,128]{2,1,0:T(8,128)(2,1)} collective-permute-done((bf16[16,128,128]{2,1,0:T(8,128)(2,1)}, bf16[16,128,128]{2,1,0:T(8,128)(2,1)}, u32[]{:S(2)}, u32[]{:S(2)}) %collective-permute-start.5) | collective-permute-done | bytes 524320 | tf_op jit(solution)/shard_map/ppermute | solution.py:314
  45.9 5.3 %collective-permute-start.6 = (bf16[16,128,128]{2,1,0:T(8,128)(2,1)}, bf16[16,128,128]{2,1,0:T(8,128)(2,1)S(1)}, u32[]{:S(2)}, u32[]{:S(2)}) collective-permute-start(bf16[16,128,128]{2,1,0:T(8,128)(2,1)} %collective-permute-done.5.refs_2_), channel_id=1, source_target_pairs={{0,112},{16,0},{32,16},{48,32},{64,48},{80,64},{96,80},{112,96},{1... | collective-permute-start | bytes 1572872 | tf_op jit(solution)/shard_map/ppermute | solution.py:314
  51.2 0.0 collective-permute-done.3.refs_1_
  51.2 1.9 %collective-permute-start.4 = (bf16[16,128,128]{2,1,0:T(8,128)(2,1)}, bf16[16,128,128]{2,1,0:T(8,128)(2,1)S(1)}, u32[]{:S(2)}, u32[]{:S(2)}) collective-permute-start(bf16[16,128,128]{2,1,0:T(8,128)(2,1)} %collective-permute-done.3.refs_1_), channel_id=1, source_target_pairs={{0,16},{16,32},{32,48},{48,64},{64,80},{80,96},{96,112},{112,0},{1... | collective-permute-start | bytes 1572872 | tf_op jit(solution)/shard_map/ppermute | solution.py:314
  53.1 3.1 %collective-permute-done.1.refs_0_ = bf16[16,128,128]{2,1,0:T(8,128)(2,1)} collective-permute-done((bf16[16,128,128]{2,1,0:T(8,128)(2,1)S(1)}, bf16[16,128,128]{2,1,0:T(8,128)(2,1)}, u32[]{:S(2)}, u32[]{:S(2)}) %collective-permute-start.1) | collective-permute-done | bytes 524320 | tf_op jit(solution)/shard_map/ppermute | solution.py:314
  56.3 1.9 %collective-permute-start.2 = (bf16[16,128,128]{2,1,0:T(8,128)(2,1)}, bf16[16,128,128]{2,1,0:T(8,128)(2,1)S(1)}, u32[]{:S(2)}, u32[]{:S(2)}) collective-permute-start(bf16[16,128,128]{2,1,0:T(8,128)(2,1)} %collective-permute-done.1.refs_0_), channel_id=1, source_target_pairs={{0,16},{16,32},{32,48},{48,64},{64,80},{80,96},{96,112},{112,0},{1... | collective-permute-start | bytes 1572872 | tf_op jit(solution)/shard_map/ppermute | solution.py:314
  58.2 0.0 collective-permute-done.8.refs_3_
  58.2 4.6 %collective-permute-start.11 = (bf16[16,128,128]{2,1,0:T(8,128)(2,1)S(1)}, bf16[16,128,128]{2,1,0:T(8,128)(2,1)S(1)}, u32[]{:S(2)}, u32[]{:S(2)}) collective-permute-start(bf16[16,128,128]{2,1,0:T(8,128)(2,1)S(1)} %collective-permute-done.8.refs_3_), channel_id=1, source_target_pairs={{0,112},{16,0},{32,16},{48,32},{64,48},{80,64},{96,80},{112,96},{1... | collective-permute-start | bytes 1572872 | tf_op jit(solution)/shard_map/ppermute | solution.py:314
  62.8 2.3 %all-gather.3.cloned.1.call-done = bf16[24832,128]{1,0:T(8,128)(2,1)} async-done(((bf16[1552,128]{1,0:T(8,128)(2,1)}), bf16[24832,128]{1,0:T(8,128)(2,1)}) %all-gather.3.cloned.1.call-update) | async-done | bytes 6357008 | tf_op jit(solution)/shard_map/all_gather | solution.py:351
  65.1 2.4 %positions.1.place_ref = s32[16,128]{1,0:T(8,128)S(1)} custom-call(bf16[16,1552,128]{2,1,0:T(8,128)(2,1)} %bitcast.9), custom_call_target="tpu_custom_call" | custom-call | flops 5000000000 | bytes 1048576 | tf_op jit(solution)/shard_map/positions/pallas_call | solution.py:142
  67.5 0.4 copy-done
  67.9 0.1 copy-done.4
  68.0 3.0 %open_sums.4 = (f32[33,128,128]{2,1,0:T(8,128)S(1)}, f32[33,128,128]{2,1,0:T(8,128)S(1)}) custom-call(s32[16,128]{1,0:T(8,128)S(1)} %positions.1.place_ref, bf16[16,1552,128]{2,1,0:T(8,128)(2,1)S(1)} %bitcast.10, bf16[16,128,128]{2,1,0:T(8,128)(2,1)S(1)} %collective-permute-done.refs_0_, bf16[16,128,128]{2,1,0:T(8,128)(2,1)} %collective-permute-done.3.refs_1_, ...), custom_call_target="tpu_custom_call" | custom-call | flops 5000000000 | bytes 1048576 | tf_op jit(solution)/shard_map/open_sums/pallas_call | solution.py:161
  71.1 0.0 copy-start.1
  71.1 5.7 %collective-permute-start.10 = (bf16[16,128,128]{2,1,0:T(8,128)(2,1)S(1)}, bf16[16,128,128]{2,1,0:T(8,128)(2,1)S(1)}, u32[]{:S(2)}, u32[]{:S(2)}) collective-permute-start(bf16[16,128,128]{2,1,0:T(8,128)(2,1)S(1)} %collective-permute-done.6.refs_2_), channel_id=1, source_target_pairs={{0,112},{16,0},{32,16},{48,32},{64,48},{80,64},{96,80},{112,96},{1... | collective-permute-start | bytes 1572872 | tf_op jit(solution)/shard_map/ppermute | solution.py:314
  76.8 0.0 collective-permute-done.4.refs_1_
  76.8 2.9 %open_sums.5 = (f32[33,128,128]{2,1,0:T(8,128)S(1)}, f32[33,128,128]{2,1,0:T(8,128)S(1)}) custom-call(s32[16,128]{1,0:T(8,128)S(1)} %positions.1.place_ref, bf16[16,1552,128]{2,1,0:T(8,128)(2,1)S(1)} %bitcast.11, bf16[16,128,128]{2,1,0:T(8,128)(2,1)} %collective-permute-done.1.refs_0_, bf16[16,128,128]{2,1,0:T(8,128)(2,1)S(1)} %collective-permute-done.4.refs_1_, ...), custom_call_target="tpu_custom_call" | custom-call | flops 5000000000 | bytes 1048576 | tf_op jit(solution)/shard_map/open_sums/pallas_call | solution.py:161
  79.7 0.0 collective-permute-done.2.refs_2_
  79.8 1.9 %collective-permute-start.9 = (bf16[16,128,128]{2,1,0:T(8,128)(2,1)S(1)}, bf16[16,128,128]{2,1,0:T(8,128)(2,1)S(1)}, u32[]{:S(2)}, u32[]{:S(2)}) collective-permute-start(bf16[16,128,128]{2,1,0:T(8,128)(2,1)S(1)} %collective-permute-done.2.refs_2_), channel_id=1, source_target_pairs={{0,16},{16,32},{32,48},{48,64},{64,80},{80,96},{96,112},{112,0},{1... | collective-permute-start | bytes 1572872 | tf_op jit(solution)/shard_map/ppermute | solution.py:314
  81.7 2.9 %open_sums.6 = (f32[33,128,128]{2,1,0:T(8,128)S(1)}, f32[33,128,128]{2,1,0:T(8,128)S(1)}) custom-call(s32[16,128]{1,0:T(8,128)S(1)} %positions.1.place_ref, bf16[16,1552,128]{2,1,0:T(8,128)(2,1)S(1)} %bitcast.12, bf16[16,128,128]{2,1,0:T(8,128)(2,1)S(1)} %copy-done.1, bf16[16,128,128]{2,1,0:T(8,128)(2,1)S(1)} %copy-done.2, ...), custom_call_target="tpu_custom_call" | custom-call | flops 5000000000 | bytes 1048576 | tf_op jit(solution)/shard_map/open_sums/pallas_call | solution.py:161
  84.6 4.6 %collective-permute-start.15 = (bf16[16,128,128]{2,1,0:T(8,128)(2,1)S(1)}, bf16[16,128,128]{2,1,0:T(8,128)(2,1)S(1)}, u32[]{:S(2)}, u32[]{:S(2)}) collective-permute-start(bf16[16,128,128]{2,1,0:T(8,128)(2,1)S(1)} %collective-permute-done.11.refs_3_), channel_id=1, source_target_pairs={{0,112},{16,0},{32,16},{48,32},{64,48},{80,64},{96,80},{112,96},{1... | collective-permute-start | bytes 1572872 | tf_op jit(solution)/shard_map/ppermute | solution.py:314
  89.2 1.9 %collective-permute-start.16 = (bf16[16,128,128]{2,1,0:T(8,128)(2,1)S(1)}, bf16[16,128,128]{2,1,0:T(8,128)(2,1)S(1)}, u32[]{:S(2)}, u32[]{:S(2)}) collective-permute-start(bf16[16,128,128]{2,1,0:T(8,128)(2,1)S(1)} %collective-permute-done.4.refs_1_), channel_id=1, source_target_pairs={{0,16},{16,32},{32,48},{48,64},{64,80},{80,96},{96,112},{112,0},{1... | collective-permute-start | bytes 1572872 | tf_op jit(solution)/shard_map/ppermute | solution.py:314
  91.1 1.4 %open_sums.7.refs_1_ = f32[33,128,128]{2,1,0:T(8,128)S(1)} custom-call(s32[16,128]{1,0:T(8,128)S(1)} %positions.1.place_ref, bf16[16,1552,128]{2,1,0:T(8,128)(2,1)S(1)} %bitcast.13, bf16[16,128,128]{2,1,0:T(8,128)(2,1)S(1)} %collective-permute-done.10.refs_0_, f32[33,128,128]{2,1,0:T(8,128)S(1)} %get-tuple-element.47.refs_1_), custom_call_target="tpu_custom_call" | custom-call | flops 5000000000 | bytes 1048576 | tf_op jit(solution)/shard_map/open_sums/pallas_call | solution.py:161
  92.5 3.3 %collective-permute-done.9.refs_0_ = bf16[16,128,128]{2,1,0:T(8,128)(2,1)S(1)} collective-permute-done((bf16[16,128,128]{2,1,0:T(8,128)(2,1)S(1)}, bf16[16,128,128]{2,1,0:T(8,128)(2,1)S(1)}, u32[]{:S(2)}, u32[]{:S(2)}) %collective-permute-start.9) | collective-permute-done | bytes 524320 | tf_op jit(solution)/shard_map/ppermute | solution.py:314
  95.8 2.4 %close_sums.2 = (f32[32,32,128]{2,1,0:T(8,128)S(1)}, s16[1056,128]{1,0:T(8,128)(2,1)S(1)}, s16[1056,128]{1,0:T(8,128)(2,1)S(1)}, s16[1056,128]{1,0:T(8,128)(2,1)S(1)}) custom-call(s32[16,128]{1,0:T(8,128)S(1)} %positions.1.place_ref, bf16[16,1552,128]{2,1,0:T(8,128)(2,1)S(1)} %bitcast.14, bf16[16,128,128]{2,1,0:T(8,128)(2,1)S(1)} %collective-permute-done.9.refs_0_, ...), custom_call_target="tpu_custom_call" | custom-call | flops 20000000000 | bytes 1048576 | tf_op jit(solution)/shard_map/close_sums/pallas_call | solution.py:161
  98.3 4.6 %collective-permute-start.12 = (s16[1056,128]{1,0:T(8,128)(2,1)S(1)}, s16[1056,128]{1,0:T(8,128)(2,1)S(1)}, u32[]{:S(2)}, u32[]{:S(2)}) collective-permute-start(s16[1056,128]{1,0:T(8,128)(2,1)S(1)} %get-tuple-element.49), channel_id=1, source_target_pairs={{0,256},{128,384},{256,0},{384,128},{1,257},{129,385},{257,1},{385... | collective-permute-start | bytes 811016 | tf_op jit(solution)/shard_map/ppermute | solution.py:314
  102.8 2.3 %collective-permute-start.13 = (s16[1056,128]{1,0:T(8,128)(2,1)S(1)}, s16[1056,128]{1,0:T(8,128)(2,1)S(1)}, u32[]{:S(2)}, u32[]{:S(2)}) collective-permute-start(s16[1056,128]{1,0:T(8,128)(2,1)S(1)} %get-tuple-element.50), channel_id=1, source_target_pairs={{0,128},{128,256},{256,384},{384,0},{1,129},{129,257},{257,385},{3... | collective-permute-start | bytes 811016 | tf_op jit(solution)/shard_map/ppermute | solution.py:314
  105.1 4.2 %collective-permute-start.14 = (s16[1056,128]{1,0:T(8,128)(2,1)S(1)}, s16[1056,128]{1,0:T(8,128)(2,1)S(1)}, u32[]{:S(2)}, u32[]{:S(2)}) collective-permute-start(s16[1056,128]{1,0:T(8,128)(2,1)S(1)} %get-tuple-element.51), channel_id=1, source_target_pairs={{0,384},{128,0},{256,128},{384,256},{1,385},{129,1},{257,129},{385... | collective-permute-start | bytes 811016 | tf_op jit(solution)/shard_map/ppermute | solution.py:314
  109.3 0.0 collective-permute-done.16.refs_1_
  109.4 3.0 %close_sums.3 = (f32[32,32,128]{2,1,0:T(8,128)S(1)}, s16[1056,128]{1,0:T(8,128)(2,1)S(1)}, s16[1056,128]{1,0:T(8,128)(2,1)S(1)}, s16[1056,128]{1,0:T(8,128)(2,1)S(1)}) custom-call(s32[16,128]{1,0:T(8,128)S(1)} %positions.1.place_ref, bf16[16,1552,128]{2,1,0:T(8,128)(2,1)S(1)} %bitcast.15, bf16[16,128,128]{2,1,0:T(8,128)(2,1)S(1)} %collective-permute-done.15.refs_0_, ...), custom_call_target="tpu_custom_call" | custom-call | flops 99999997952 | bytes 1048576 | tf_op jit(solution)/shard_map/close_sums/pallas_call | solution.py:161
  112.3 2.3 %collective-permute-start.17 = (s16[1056,128]{1,0:T(8,128)(2,1)S(1)}, s16[1056,128]{1,0:T(8,128)(2,1)S(1)}, u32[]{:S(2)}, u32[]{:S(2)}) collective-permute-start(s16[1056,128]{1,0:T(8,128)(2,1)S(1)} %get-tuple-element.56), channel_id=1, source_target_pairs={{0,256},{128,384},{256,0},{384,128},{1,257},{129,385},{257,1},{385... | collective-permute-start | bytes 811016 | tf_op jit(solution)/shard_map/ppermute | solution.py:314
  114.6 2.3 %collective-permute-start.18 = (s16[1056,128]{1,0:T(8,128)(2,1)S(1)}, s16[1056,128]{1,0:T(8,128)(2,1)S(1)}, u32[]{:S(2)}, u32[]{:S(2)}) collective-permute-start(s16[1056,128]{1,0:T(8,128)(2,1)S(1)} %get-tuple-element.57), channel_id=1, source_target_pairs={{0,128},{128,256},{256,384},{384,0},{1,129},{129,257},{257,385},{3... | collective-permute-start | bytes 811016 | tf_op jit(solution)/shard_map/ppermute | solution.py:314
  116.9 0.0 collective-permute-done.12.refs_0_
  116.9 4.2 %collective-permute-start.19 = (s16[1056,128]{1,0:T(8,128)(2,1)S(1)}, s16[1056,128]{1,0:T(8,128)(2,1)S(1)}, u32[]{:S(2)}, u32[]{:S(2)}) collective-permute-start(s16[1056,128]{1,0:T(8,128)(2,1)S(1)} %get-tuple-element.58), channel_id=1, source_target_pairs={{0,384},{128,0},{256,128},{384,256},{1,385},{129,1},{257,129},{385... | collective-permute-start | bytes 811016 | tf_op jit(solution)/shard_map/ppermute | solution.py:314
  121.1 0.4 first_combine.1.first_ref
  121.6 0.0 collective-permute-done.17.refs_0_
  121.6 6.7 %collective-permute-done.18.refs_1_ = s16[1056,128]{1,0:T(8,128)(2,1)S(1)} collective-permute-done((s16[1056,128]{1,0:T(8,128)(2,1)S(1)}, s16[1056,128]{1,0:T(8,128)(2,1)S(1)}, u32[]{:S(2)}, u32[]{:S(2)}) %collective-permute-start.18) | collective-permute-done | bytes 270368 | tf_op jit(solution)/shard_map/ppermute | solution.py:314
  128.3 2.1 %last_combine.1 = f32[2048,128]{1,0:T(8,128)} custom-call(f32[32,32,128]{2,1,0:T(8,128)S(1)} %first_combine.1.first_ref, f32[32,32,128]{2,1,0:T(8,128)S(1)} %get-tuple-element.55.own_ref, s16[1056,128]{1,0:T(8,128)(2,1)S(1)} %collective-permute-done.17.refs_0_, s16[1056,128]{1,0:T(8,128)(2,1)S(1)} %collective-permute-done.18.refs_1_, ...), custom_call_target="tpu_custom_call" | custom-call | flops 1000000000 | bytes 1048576 | tf_op jit(solution)/shard_map/last_combine/pallas_call | solution.py:241
  (15 shorter events, 0.0 us)
Async XLA Ops:
  6.5 58.6 %all-gather.3.cloned.1.call-start = ((), (), s32[]{:S(2)}) async-start(), calls=%async_computation | async-start | bytes 6754304 | tf_op jit(solution)/shard_map/all_gather | solution.py:351
  10.3 23.3 %collective-permute-start = (bf16[16,128,128]{2,1,0:T(8,128)(2,1)}, bf16[16,128,128]{2,1,0:T(8,128)(2,1)S(1)}, u32[]{:S(2)}, u32[]{:S(2)}) collective-permute-start(bf16[16,128,128]{2,1,0:T(8,128)(2,1)} %get-tuple-element.33.refs_0_), channel_id=1, source_target_pairs={{0,16},{16,32},{32,48},{48,64},{64,80},{80,96},{96,112},{112,0},{1... | collective-permute-start | bytes 1572872 | tf_op jit(solution)/shard_map/ppermute | solution.py:314
  15.2 20.4 %collective-permute-start.7 = (bf16[16,128,128]{2,1,0:T(8,128)(2,1)}, bf16[16,128,128]{2,1,0:T(8,128)(2,1)S(1)}, u32[]{:S(2)}, u32[]{:S(2)}) collective-permute-start(bf16[16,128,128]{2,1,0:T(8,128)(2,1)} %get-tuple-element.34.refs_1_), channel_id=1, source_target_pairs={{0,112},{16,0},{32,16},{48,32},{64,48},{80,64},{96,80},{112,96},{1... | collective-permute-start | bytes 1572872 | tf_op jit(solution)/shard_map/ppermute | solution.py:314
  23.8 22.1 %collective-permute-start.5 = (bf16[16,128,128]{2,1,0:T(8,128)(2,1)}, bf16[16,128,128]{2,1,0:T(8,128)(2,1)}, u32[]{:S(2)}, u32[]{:S(2)}) collective-permute-start(bf16[16,128,128]{2,1,0:T(8,128)(2,1)} %get-tuple-element.33.refs_0_), channel_id=1, source_target_pairs={{0,112},{16,0},{32,16},{48,32},{64,48},{80,64},{96,80},{112,96},{1... | collective-permute-start | bytes 1572872 | tf_op jit(solution)/shard_map/ppermute | solution.py:314
  27.1 24.1 %collective-permute-start.3 = (bf16[16,128,128]{2,1,0:T(8,128)(2,1)}, bf16[16,128,128]{2,1,0:T(8,128)(2,1)}, u32[]{:S(2)}, u32[]{:S(2)}) collective-permute-start(bf16[16,128,128]{2,1,0:T(8,128)(2,1)} %get-tuple-element.34.refs_1_), channel_id=1, source_target_pairs={{0,16},{16,32},{32,48},{48,64},{64,80},{80,96},{96,112},{112,0},{1... | collective-permute-start | bytes 1572872 | tf_op jit(solution)/shard_map/ppermute | solution.py:314
  33.7 22.6 %collective-permute-start.1 = (bf16[16,128,128]{2,1,0:T(8,128)(2,1)S(1)}, bf16[16,128,128]{2,1,0:T(8,128)(2,1)}, u32[]{:S(2)}, u32[]{:S(2)}) collective-permute-start(bf16[16,128,128]{2,1,0:T(8,128)(2,1)S(1)} %collective-permute-done.refs_0_), channel_id=1, source_target_pairs={{0,16},{16,32},{32,48},{48,64},{64,80},{80,96},{96,112},{112,0},{1... | collective-permute-start | bytes 1572872 | tf_op jit(solution)/shard_map/ppermute | solution.py:314
  35.6 22.6 %collective-permute-start.8 = (bf16[16,128,128]{2,1,0:T(8,128)(2,1)S(1)}, bf16[16,128,128]{2,1,0:T(8,128)(2,1)S(1)}, u32[]{:S(2)}, u32[]{:S(2)}) collective-permute-start(bf16[16,128,128]{2,1,0:T(8,128)(2,1)S(1)} %collective-permute-done.7.refs_3_), channel_id=1, source_target_pairs={{0,112},{16,0},{32,16},{48,32},{64,48},{80,64},{96,80},{112,96},{1... | collective-permute-start | bytes 1572872 | tf_op jit(solution)/shard_map/ppermute | solution.py:314
  40.2 0.8 copy-start.3
  45.9 25.2 %collective-permute-start.6 = (bf16[16,128,128]{2,1,0:T(8,128)(2,1)}, bf16[16,128,128]{2,1,0:T(8,128)(2,1)S(1)}, u32[]{:S(2)}, u32[]{:S(2)}) collective-permute-start(bf16[16,128,128]{2,1,0:T(8,128)(2,1)} %collective-permute-done.5.refs_2_), channel_id=1, source_target_pairs={{0,112},{16,0},{32,16},{48,32},{64,48},{80,64},{96,80},{112,96},{1... | collective-permute-start | bytes 1572872 | tf_op jit(solution)/shard_map/ppermute | solution.py:314
  51.2 25.6 %collective-permute-start.4 = (bf16[16,128,128]{2,1,0:T(8,128)(2,1)}, bf16[16,128,128]{2,1,0:T(8,128)(2,1)S(1)}, u32[]{:S(2)}, u32[]{:S(2)}) collective-permute-start(bf16[16,128,128]{2,1,0:T(8,128)(2,1)} %collective-permute-done.3.refs_1_), channel_id=1, source_target_pairs={{0,16},{16,32},{32,48},{48,64},{64,80},{80,96},{96,112},{112,0},{1... | collective-permute-start | bytes 1572872 | tf_op jit(solution)/shard_map/ppermute | solution.py:314
  56.3 23.5 %collective-permute-start.2 = (bf16[16,128,128]{2,1,0:T(8,128)(2,1)}, bf16[16,128,128]{2,1,0:T(8,128)(2,1)S(1)}, u32[]{:S(2)}, u32[]{:S(2)}) collective-permute-start(bf16[16,128,128]{2,1,0:T(8,128)(2,1)} %collective-permute-done.1.refs_0_), channel_id=1, source_target_pairs={{0,16},{16,32},{32,48},{48,64},{64,80},{80,96},{96,112},{112,0},{1... | collective-permute-start | bytes 1572872 | tf_op jit(solution)/shard_map/ppermute | solution.py:314
  58.2 23.5 %collective-permute-start.11 = (bf16[16,128,128]{2,1,0:T(8,128)(2,1)S(1)}, bf16[16,128,128]{2,1,0:T(8,128)(2,1)S(1)}, u32[]{:S(2)}, u32[]{:S(2)}) collective-permute-start(bf16[16,128,128]{2,1,0:T(8,128)(2,1)S(1)} %collective-permute-done.8.refs_3_), channel_id=1, source_target_pairs={{0,112},{16,0},{32,16},{48,32},{64,48},{80,64},{96,80},{112,96},{1... | collective-permute-start | bytes 1572872 | tf_op jit(solution)/shard_map/ppermute | solution.py:314
  65.1 2.8 %copy-start = (bf16[24832,128]{1,0:T(8,128)(2,1)S(1)}, bf16[24832,128]{1,0:T(8,128)(2,1)}, u32[]{:S(2)}) copy-start(bf16[24832,128]{1,0:T(8,128)(2,1)} %all-gather.3.cloned.1.call-done) | copy-start | bytes 19070980
  65.1 2.9 %copy-start.4 = (bf16[16,128,128]{2,1,0:T(8,128)(2,1)S(1)}, bf16[16,128,128]{2,1,0:T(8,128)(2,1)}, u32[]{:S(2)}) copy-start(bf16[16,128,128]{2,1,0:T(8,128)(2,1)} %copy-done.3) | copy-start | bytes 1572868
  71.1 10.6 %copy-start.1 = (bf16[16,128,128]{2,1,0:T(8,128)(2,1)S(1)}, bf16[16,128,128]{2,1,0:T(8,128)(2,1)}, u32[]{:S(2)}) copy-start(bf16[16,128,128]{2,1,0:T(8,128)(2,1)} %get-tuple-element.33.refs_0_) | copy-start | bytes 1572868
  71.1 10.6 %copy-start.2 = (bf16[16,128,128]{2,1,0:T(8,128)(2,1)S(1)}, bf16[16,128,128]{2,1,0:T(8,128)(2,1)}, u32[]{:S(2)}) copy-start(bf16[16,128,128]{2,1,0:T(8,128)(2,1)} %get-tuple-element.34.refs_1_) | copy-start | bytes 1572868
  71.1 20.0 %collective-permute-start.10 = (bf16[16,128,128]{2,1,0:T(8,128)(2,1)S(1)}, bf16[16,128,128]{2,1,0:T(8,128)(2,1)S(1)}, u32[]{:S(2)}, u32[]{:S(2)}) collective-permute-start(bf16[16,128,128]{2,1,0:T(8,128)(2,1)S(1)} %collective-permute-done.6.refs_2_), channel_id=1, source_target_pairs={{0,112},{16,0},{32,16},{48,32},{64,48},{80,64},{96,80},{112,96},{1... | collective-permute-start | bytes 1572872 | tf_op jit(solution)/shard_map/ppermute | solution.py:314
  79.8 16.1 %collective-permute-start.9 = (bf16[16,128,128]{2,1,0:T(8,128)(2,1)S(1)}, bf16[16,128,128]{2,1,0:T(8,128)(2,1)S(1)}, u32[]{:S(2)}, u32[]{:S(2)}) collective-permute-start(bf16[16,128,128]{2,1,0:T(8,128)(2,1)S(1)} %collective-permute-done.2.refs_2_), channel_id=1, source_target_pairs={{0,16},{16,32},{32,48},{48,64},{64,80},{80,96},{96,112},{112,0},{1... | collective-permute-start | bytes 1572872 | tf_op jit(solution)/shard_map/ppermute | solution.py:314
  84.6 24.8 %collective-permute-start.15 = (bf16[16,128,128]{2,1,0:T(8,128)(2,1)S(1)}, bf16[16,128,128]{2,1,0:T(8,128)(2,1)S(1)}, u32[]{:S(2)}, u32[]{:S(2)}) collective-permute-start(bf16[16,128,128]{2,1,0:T(8,128)(2,1)S(1)} %collective-permute-done.11.refs_3_), channel_id=1, source_target_pairs={{0,112},{16,0},{32,16},{48,32},{64,48},{80,64},{96,80},{112,96},{1... | collective-permute-start | bytes 1572872 | tf_op jit(solution)/shard_map/ppermute | solution.py:314
  89.2 20.2 %collective-permute-start.16 = (bf16[16,128,128]{2,1,0:T(8,128)(2,1)S(1)}, bf16[16,128,128]{2,1,0:T(8,128)(2,1)S(1)}, u32[]{:S(2)}, u32[]{:S(2)}) collective-permute-start(bf16[16,128,128]{2,1,0:T(8,128)(2,1)S(1)} %collective-permute-done.4.refs_1_), channel_id=1, source_target_pairs={{0,16},{16,32},{32,48},{48,64},{64,80},{80,96},{96,112},{112,0},{1... | collective-permute-start | bytes 1572872 | tf_op jit(solution)/shard_map/ppermute | solution.py:314
  98.3 18.6 %collective-permute-start.12 = (s16[1056,128]{1,0:T(8,128)(2,1)S(1)}, s16[1056,128]{1,0:T(8,128)(2,1)S(1)}, u32[]{:S(2)}, u32[]{:S(2)}) collective-permute-start(s16[1056,128]{1,0:T(8,128)(2,1)S(1)} %get-tuple-element.49), channel_id=1, source_target_pairs={{0,256},{128,384},{256,0},{384,128},{1,257},{129,385},{257,1},{385... | collective-permute-start | bytes 811016 | tf_op jit(solution)/shard_map/ppermute | solution.py:314
  102.8 18.3 %collective-permute-start.13 = (s16[1056,128]{1,0:T(8,128)(2,1)S(1)}, s16[1056,128]{1,0:T(8,128)(2,1)S(1)}, u32[]{:S(2)}, u32[]{:S(2)}) collective-permute-start(s16[1056,128]{1,0:T(8,128)(2,1)S(1)} %get-tuple-element.50), channel_id=1, source_target_pairs={{0,128},{128,256},{256,384},{384,0},{1,129},{129,257},{257,385},{3... | collective-permute-start | bytes 811016 | tf_op jit(solution)/shard_map/ppermute | solution.py:314
  105.1 16.0 %collective-permute-start.14 = (s16[1056,128]{1,0:T(8,128)(2,1)S(1)}, s16[1056,128]{1,0:T(8,128)(2,1)S(1)}, u32[]{:S(2)}, u32[]{:S(2)}) collective-permute-start(s16[1056,128]{1,0:T(8,128)(2,1)S(1)} %get-tuple-element.51), channel_id=1, source_target_pairs={{0,384},{128,0},{256,128},{384,256},{1,385},{129,1},{257,129},{385... | collective-permute-start | bytes 811016 | tf_op jit(solution)/shard_map/ppermute | solution.py:314
  112.3 9.2 %collective-permute-start.17 = (s16[1056,128]{1,0:T(8,128)(2,1)S(1)}, s16[1056,128]{1,0:T(8,128)(2,1)S(1)}, u32[]{:S(2)}, u32[]{:S(2)}) collective-permute-start(s16[1056,128]{1,0:T(8,128)(2,1)S(1)} %get-tuple-element.56), channel_id=1, source_target_pairs={{0,256},{128,384},{256,0},{384,128},{1,257},{129,385},{257,1},{385... | collective-permute-start | bytes 811016 | tf_op jit(solution)/shard_map/ppermute | solution.py:314
  114.6 13.7 %collective-permute-start.18 = (s16[1056,128]{1,0:T(8,128)(2,1)S(1)}, s16[1056,128]{1,0:T(8,128)(2,1)S(1)}, u32[]{:S(2)}, u32[]{:S(2)}) collective-permute-start(s16[1056,128]{1,0:T(8,128)(2,1)S(1)} %get-tuple-element.57), channel_id=1, source_target_pairs={{0,128},{128,256},{256,384},{384,0},{1,129},{129,257},{257,385},{3... | collective-permute-start | bytes 811016 | tf_op jit(solution)/shard_map/ppermute | solution.py:314
  116.9 11.4 %collective-permute-start.19 = (s16[1056,128]{1,0:T(8,128)(2,1)S(1)}, s16[1056,128]{1,0:T(8,128)(2,1)S(1)}, u32[]{:S(2)}, u32[]{:S(2)}) collective-permute-start(s16[1056,128]{1,0:T(8,128)(2,1)S(1)} %get-tuple-element.58), channel_id=1, source_target_pairs={{0,384},{128,0},{256,128},{384,256},{1,385},{129,1},{257,129},{385... | collective-permute-start | bytes 811016 | tf_op jit(solution)/shard_map/ppermute | solution.py:314
Sparse Core Ops, SparseCore 0:
  10.5 54.5 all-gather.2

commit v3 on v0

--- a/solution.py
+++ b/solution.py
@@ -80,7 +80,7 @@
             outs[c][i] = refs[c][i] if resumed else jnp.zeros((BS, BS), jnp.float32)
         return carry
 
-    lax.fori_loop(0, RB_DEV, load, 0)
+    lax.fori_loop(0, RB_DEV, load, 0, unroll=4)
     add_both(place_ref, a_ref, both, outs, pairs)
     for c in range(width):
         add_products(place_ref, a_ref, alone[c], outs[c], singles[c])
@@ -97,7 +97,7 @@
         acc[i] = before_ref[i]
         return carry
 
-    lax.fori_loop(0, RB_DEV, load, 0)
+    lax.fori_loop(0, RB_DEV, load, 0, unroll=4)
     add_products(place_ref, a_ref, places, acc, refs[:count])
 
     def keep(i, carry):
@@ -108,7 +108,7 @@
             top[q - 1, pl.ds(i, 1), :] = jnp.max(jnp.abs(part), axis=0, keepdims=True)
         return carry
 
-    lax.fori_loop(0, RB_DEV, keep, 0)
+    lax.fori_loop(0, RB_DEV, keep, 0, unroll=4)
     for q in range(1, N_LAYER):
         power = jnp.floor(jnp.log(jnp.maximum(top[q - 1], 1e-30)) * (1.0 / LN2))
         msg_refs[q - 1][pl.ds(RB_DEV * XQ, RB_DEV), :] = power.astype(jnp.int32).astype(jnp.int16)
@@ -123,7 +123,7 @@
             )
         return carry
 
-    lax.fori_loop(0, RB_DEV, pack, 0)
+    lax.fori_loop(0, RB_DEV, pack, 0, unroll=4)
 
 
 def positions_kernel(a_ref, place_ref, held, place, sem):
@@ -221,7 +221,7 @@
         out_ref[i] = add_messages(own_ref, msgs, scale, i)
         return carry
 
-    lax.fori_loop(0, RB_DEV, step, 0)
+    lax.fori_loop(0, RB_DEV, step, 0, unroll=4)
 
 
 def last_combine_kernel(first_ref, own_ref, *refs):
@@ -233,7 +233,7 @@
         out_ref[pl.ds(CB_DEV * i + 1, XQ, stride=RB_DEV * CB_DEV), :] = add_messages(own_ref, msgs, scale, i)
         return carry
 
-    lax.fori_loop(0, RB_DEV, step, 0)
+    lax.fori_loop(0, RB_DEV, step, 0, unroll=4)
 
 
 def combine(kernel, shape, parts, name):

time: 136 us -> 135 us (level)
  Pallas kernels: 22.7 us -> 21.2 us
  transfers between devices with their start and end apart: 21 -> 21, of which waited for: 7 -> 8; matrix products, arithmetic and copies ran while one was open for 0% -> 0% of each run, Pallas kernels for 13% -> 12%
where the time goes in v3:
time: 135 us; the launch traced here: 133 us
  starting transfers between devices  72.7 us (54%)
  waiting for transfers between devices  23.5 us (17%)
  Pallas kernels  21.2 us (16%)
  between operations  14.4 us (11%)
    ppermute x20, starting transfers between devices, shifted(): lax.ppermute(value, axis, [(i, (i + by) % size) for i in range(size)])  72.7 us
    ppermute x20, waiting for transfers between devices, shifted(): lax.ppermute(value, axis, [(i, (i + by) % size) for i in range(size)])  21.2 us
    pallas_call x5, Pallas kernels, call_products(): pl.pallas_call(kernel, out_shape=out_shape, in_specs=[smem] + [vmem] * (l...  13.4 us
    pallas_call x1, Pallas kernels, prepare(): pl.pallas_call(prepare_kernel, out_shape=[a_send, chunk, chunk], in_specs...  3.12 us
  transfers between devices with their start and end apart: 21, of which 8 were waited for; matrix products, arithmetic and copies ran while one was open for 0% of the time, Pallas kernels for 12%

profile of v3, /device:TPU:1, one launch (start us, length us, event | category | flops | bytes accessed | tf_op | source)
XLA Modules:
  0.0 132.7 jit_solution(779592804757836150)
XLA Ops:
  7.2 3.1 %prepare.1 = (bf16[1552,128]{1,0:T(8,128)(2,1)}, bf16[16,128,128]{2,1,0:T(8,128)(2,1)}, bf16[16,128,128]{2,1,0:T(8,128)(2,1)}) custom-call(bf16[1536,128]{1,0:T(8,128)(2,1)} %bitcast.16, s32[12]{0:T(128)} %bitcast.18, s32[12]{0:T(128)} %bitcast.19, s32[1,1,1]{2,1,0:T(1,128)S(6)} %copy.7.live_ref, bf16[16,2,128,128]{3,2,1,0:T(8,128)(2,1)} %bitcast.15, ...), custom_call_target="tpu_custom_call" | custom-call | tf_op jit(solution)/shard_map/prepare/pallas_call | solution.py:289
  10.3 0.0 all-gather.3.cloned.1.call-update
  10.3 4.9 %collective-permute-start.2 = (bf16[16,128,128]{2,1,0:T(8,128)(2,1)}, bf16[16,128,128]{2,1,0:T(8,128)(2,1)S(1)}, u32[]{:S(2)}, u32[]{:S(2)}) collective-permute-start(bf16[16,128,128]{2,1,0:T(8,128)(2,1)} %get-tuple-element.29.refs_4_), channel_id=1, source_target_pairs={{0,16},{16,32},{32,48},{48,64},{64,80},{80,96},{96,112},{112,0},{1... | collective-permute-start | bytes 1572872 | tf_op jit(solution)/shard_map/ppermute | solution.py:314
  15.2 8.6 %collective-permute-start.6 = (bf16[16,128,128]{2,1,0:T(8,128)(2,1)}, bf16[16,128,128]{2,1,0:T(8,128)(2,1)S(1)}, u32[]{:S(2)}, u32[]{:S(2)}) collective-permute-start(bf16[16,128,128]{2,1,0:T(8,128)(2,1)} %get-tuple-element.32.refs_5_), channel_id=1, source_target_pairs={{0,112},{16,0},{32,16},{48,32},{64,48},{80,64},{96,80},{112,96},{1... | collective-permute-start | bytes 1572872 | tf_op jit(solution)/shard_map/ppermute | solution.py:314
  23.8 3.4 %collective-permute-start = (bf16[16,128,128]{2,1,0:T(8,128)(2,1)}, bf16[16,128,128]{2,1,0:T(8,128)(2,1)}, u32[]{:S(2)}, u32[]{:S(2)}) collective-permute-start(bf16[16,128,128]{2,1,0:T(8,128)(2,1)} %get-tuple-element.29.refs_4_), channel_id=1, source_target_pairs={{0,112},{16,0},{32,16},{48,32},{64,48},{80,64},{96,80},{112,96},{1... | collective-permute-start | bytes 1572872 | tf_op jit(solution)/shard_map/ppermute | solution.py:314
  27.1 1.9 %collective-permute-start.5 = (bf16[16,128,128]{2,1,0:T(8,128)(2,1)}, bf16[16,128,128]{2,1,0:T(8,128)(2,1)S(1)}, u32[]{:S(2)}, u32[]{:S(2)}) collective-permute-start(bf16[16,128,128]{2,1,0:T(8,128)(2,1)} %get-tuple-element.32.refs_5_), channel_id=1, source_target_pairs={{0,16},{16,32},{32,48},{48,64},{64,80},{80,96},{96,112},{112,0},{1... | collective-permute-start | bytes 1572872 | tf_op jit(solution)/shard_map/ppermute | solution.py:314
  29.1 4.6 %collective-permute-done.2.refs_0_ = bf16[16,128,128]{2,1,0:T(8,128)(2,1)S(1)} collective-permute-done((bf16[16,128,128]{2,1,0:T(8,128)(2,1)}, bf16[16,128,128]{2,1,0:T(8,128)(2,1)S(1)}, u32[]{:S(2)}, u32[]{:S(2)}) %collective-permute-start.2) | collective-permute-done | bytes 524320 | tf_op jit(solution)/shard_map/ppermute | solution.py:314
  33.7 1.9 %collective-permute-start.3 = (bf16[16,128,128]{2,1,0:T(8,128)(2,1)S(1)}, bf16[16,128,128]{2,1,0:T(8,128)(2,1)S(1)}, u32[]{:S(2)}, u32[]{:S(2)}) collective-permute-start(bf16[16,128,128]{2,1,0:T(8,128)(2,1)S(1)} %collective-permute-done.2.refs_0_), channel_id=1, source_target_pairs={{0,16},{16,32},{32,48},{48,64},{64,80},{80,96},{96,112},{112,0},{1... | collective-permute-start | bytes 1572872 | tf_op jit(solution)/shard_map/ppermute | solution.py:314
  35.6 0.0 collective-permute-done.6.refs_3_
  35.6 4.6 %collective-permute-start.9 = (bf16[16,128,128]{2,1,0:T(8,128)(2,1)S(1)}, bf16[16,128,128]{2,1,0:T(8,128)(2,1)}, u32[]{:S(2)}, u32[]{:S(2)}) collective-permute-start(bf16[16,128,128]{2,1,0:T(8,128)(2,1)S(1)} %collective-permute-done.6.refs_3_), channel_id=1, source_target_pairs={{0,112},{16,0},{32,16},{48,32},{64,48},{80,64},{96,80},{112,96},{1... | collective-permute-start | bytes 1572872 | tf_op jit(solution)/shard_map/ppermute | solution.py:314
  40.2 0.8 copy-done.3
  41.0 4.9 %collective-permute-done.refs_2_ = bf16[16,128,128]{2,1,0:T(8,128)(2,1)} collective-permute-done((bf16[16,128,128]{2,1,0:T(8,128)(2,1)}, bf16[16,128,128]{2,1,0:T(8,128)(2,1)}, u32[]{:S(2)}, u32[]{:S(2)}) %collective-permute-start) | collective-permute-done | bytes 524320 | tf_op jit(solution)/shard_map/ppermute | solution.py:314
  45.9 5.3 %collective-permute-start.1 = (bf16[16,128,128]{2,1,0:T(8,128)(2,1)}, bf16[16,128,128]{2,1,0:T(8,128)(2,1)S(1)}, u32[]{:S(2)}, u32[]{:S(2)}) collective-permute-start(bf16[16,128,128]{2,1,0:T(8,128)(2,1)} %collective-permute-done.refs_2_), channel_id=1, source_target_pairs={{0,112},{16,0},{32,16},{48,32},{64,48},{80,64},{96,80},{112,96},{1... | collective-permute-start | bytes 1572872 | tf_op jit(solution)/shard_map/ppermute | solution.py:314
  51.2 0.0 collective-permute-done.5.refs_1_
  51.2 1.9 %collective-permute-start.11 = (bf16[16,128,128]{2,1,0:T(8,128)(2,1)S(1)}, bf16[16,128,128]{2,1,0:T(8,128)(2,1)S(1)}, u32[]{:S(2)}, u32[]{:S(2)}) collective-permute-start(bf16[16,128,128]{2,1,0:T(8,128)(2,1)S(1)} %collective-permute-done.5.refs_1_), channel_id=1, source_target_pairs={{0,16},{16,32},{32,48},{48,64},{64,80},{80,96},{96,112},{112,0},{1... | collective-permute-start | bytes 1572872 | tf_op jit(solution)/shard_map/ppermute | solution.py:314
  53.1 3.1 %collective-permute-done.3.refs_0_ = bf16[16,128,128]{2,1,0:T(8,128)(2,1)S(1)} collective-permute-done((bf16[16,128,128]{2,1,0:T(8,128)(2,1)S(1)}, bf16[16,128,128]{2,1,0:T(8,128)(2,1)S(1)}, u32[]{:S(2)}, u32[]{:S(2)}) %collective-permute-start.3) | collective-permute-done | bytes 524320 | tf_op jit(solution)/shard_map/ppermute | solution.py:314
  56.3 1.9 %collective-permute-start.4 = (bf16[16,128,128]{2,1,0:T(8,128)(2,1)S(1)}, bf16[16,128,128]{2,1,0:T(8,128)(2,1)}, u32[]{:S(2)}, u32[]{:S(2)}) collective-permute-start(bf16[16,128,128]{2,1,0:T(8,128)(2,1)S(1)} %collective-permute-done.3.refs_0_), channel_id=1, source_target_pairs={{0,16},{16,32},{32,48},{48,64},{64,80},{80,96},{96,112},{112,0},{1... | collective-permute-start | bytes 1572872 | tf_op jit(solution)/shard_map/ppermute | solution.py:314
  58.2 4.6 %collective-permute-start.10 = (bf16[16,128,128]{2,1,0:T(8,128)(2,1)}, bf16[16,128,128]{2,1,0:T(8,128)(2,1)S(1)}, u32[]{:S(2)}, u32[]{:S(2)}) collective-permute-start(bf16[16,128,128]{2,1,0:T(8,128)(2,1)} %collective-permute-done.9.refs_3_), channel_id=1, source_target_pairs={{0,112},{16,0},{32,16},{48,32},{64,48},{80,64},{96,80},{112,96},{1... | collective-permute-start | bytes 1572872 | tf_op jit(solution)/shard_map/ppermute | solution.py:314
  62.8 2.3 %all-gather.3.cloned.1.call-done = bf16[24832,128]{1,0:T(8,128)(2,1)} async-done(((bf16[1552,128]{1,0:T(8,128)(2,1)}), bf16[24832,128]{1,0:T(8,128)(2,1)}) %all-gather.3.cloned.1.call-update) | async-done | bytes 6357008 | tf_op jit(solution)/shard_map/all_gather | solution.py:351
  65.1 2.4 %positions.1.place_ref = s32[16,128]{1,0:T(8,128)S(1)} custom-call(bf16[16,1552,128]{2,1,0:T(8,128)(2,1)} %bitcast.9), custom_call_target="tpu_custom_call" | custom-call | flops 5000000000 | bytes 1048576 | tf_op jit(solution)/shard_map/positions/pallas_call | solution.py:142
  67.5 0.0 copy-start.1
  67.5 0.8 collective-permute-done.1.refs_2_
  68.4 5.2 %collective-permute-start.8 = (bf16[16,128,128]{2,1,0:T(8,128)(2,1)S(1)}, bf16[16,128,128]{2,1,0:T(8,128)(2,1)S(1)}, u32[]{:S(2)}, u32[]{:S(2)}) collective-permute-start(bf16[16,128,128]{2,1,0:T(8,128)(2,1)S(1)} %collective-permute-done.1.refs_2_), channel_id=1, source_target_pairs={{0,112},{16,0},{32,16},{48,32},{64,48},{80,64},{96,80},{112,96},{1... | collective-permute-start | bytes 1572872 | tf_op jit(solution)/shard_map/ppermute | solution.py:314
  73.6 2.8 %open_sums.3 = (f32[33,128,128]{2,1,0:T(8,128)S(1)}, f32[33,128,128]{2,1,0:T(8,128)S(1)}) custom-call(s32[16,128]{1,0:T(8,128)S(1)} %positions.1.place_ref, bf16[16,1552,128]{2,1,0:T(8,128)(2,1)S(1)} %bitcast.10, bf16[16,128,128]{2,1,0:T(8,128)(2,1)S(1)} %collective-permute-done.2.refs_0_, bf16[16,128,128]{2,1,0:T(8,128)(2,1)S(1)} %collective-permute-done.5.refs_1_, ...), custom_call_target="tpu_custom_call" | custom-call | flops 5000000000 | bytes 1048576 | tf_op jit(solution)/shard_map/open_sums/pallas_call | solution.py:161
  76.4 0.0 collective-permute-done.4.refs_6_
  76.5 1.9 %collective-permute-start.7 = (bf16[16,128,128]{2,1,0:T(8,128)(2,1)}, bf16[16,128,128]{2,1,0:T(8,128)(2,1)S(1)}, u32[]{:S(2)}, u32[]{:S(2)}) collective-permute-start(bf16[16,128,128]{2,1,0:T(8,128)(2,1)} %collective-permute-done.4.refs_6_), channel_id=1, source_target_pairs={{0,16},{16,32},{32,48},{48,64},{64,80},{80,96},{96,112},{112,0},{1... | collective-permute-start | bytes 1572872 | tf_op jit(solution)/shard_map/ppermute | solution.py:314
  78.4 0.0 collective-permute-done.11.refs_1_
  78.4 1.2 collective-permute-done.10.refs_7_
  79.6 4.9 %open_sums.4 = (f32[33,128,128]{2,1,0:T(8,128)S(1)}, f32[33,128,128]{2,1,0:T(8,128)S(1)}) custom-call(s32[16,128]{1,0:T(8,128)S(1)} %positions.1.place_ref, bf16[16,1552,128]{2,1,0:T(8,128)(2,1)S(1)} %bitcast.11, bf16[16,128,128]{2,1,0:T(8,128)(2,1)S(1)} %collective-permute-done.3.refs_0_, bf16[16,128,128]{2,1,0:T(8,128)(2,1)S(1)} %collective-permute-done.11.refs_1_, ...), custom_call_target="tpu_custom_call" | custom-call | flops 5000000000 | bytes 1048576 | tf_op jit(solution)/shard_map/open_sums/pallas_call | solution.py:161
  84.5 5.2 %collective-permute-start.15 = (bf16[16,128,128]{2,1,0:T(8,128)(2,1)S(1)}, bf16[16,128,128]{2,1,0:T(8,128)(2,1)S(1)}, u32[]{:S(2)}, u32[]{:S(2)}) collective-permute-start(bf16[16,128,128]{2,1,0:T(8,128)(2,1)S(1)} %collective-permute-done.10.refs_7_), channel_id=1, source_target_pairs={{0,112},{16,0},{32,16},{48,32},{64,48},{80,64},{96,80},{112,96},{1... | collective-permute-start | bytes 1572872 | tf_op jit(solution)/shard_map/ppermute | solution.py:314
  89.7 1.9 %collective-permute-start.16 = (bf16[16,128,128]{2,1,0:T(8,128)(2,1)S(1)}, bf16[16,128,128]{2,1,0:T(8,128)(2,1)S(1)}, u32[]{:S(2)}, u32[]{:S(2)}) collective-permute-start(bf16[16,128,128]{2,1,0:T(8,128)(2,1)S(1)} %collective-permute-done.11.refs_1_), channel_id=1, source_target_pairs={{0,16},{16,32},{32,48},{48,64},{64,80},{80,96},{96,112},{112,0},{1... | collective-permute-start | bytes 1572872 | tf_op jit(solution)/shard_map/ppermute | solution.py:314
  91.6 0.0 collective-permute-done.8.refs_0_
  91.7 1.4 %open_sums.5.refs_1_ = f32[33,128,128]{2,1,0:T(8,128)S(1)} custom-call(s32[16,128]{1,0:T(8,128)S(1)} %positions.1.place_ref, bf16[16,1552,128]{2,1,0:T(8,128)(2,1)S(1)} %bitcast.12, bf16[16,128,128]{2,1,0:T(8,128)(2,1)S(1)} %collective-permute-done.8.refs_0_, f32[33,128,128]{2,1,0:T(8,128)S(1)} %get-tuple-element.41.refs_1_), custom_call_target="tpu_custom_call" | custom-call | flops 5000000000 | bytes 1048576 | tf_op jit(solution)/shard_map/open_sums/pallas_call | solution.py:161
  93.0 1.9 %close_sums.2 = (f32[32,32,128]{2,1,0:T(8,128)S(1)}, s16[1056,128]{1,0:T(8,128)(2,1)S(1)}, s16[1056,128]{1,0:T(8,128)(2,1)S(1)}, s16[1056,128]{1,0:T(8,128)(2,1)S(1)}) custom-call(s32[16,128]{1,0:T(8,128)S(1)} %positions.1.place_ref, bf16[16,1552,128]{2,1,0:T(8,128)(2,1)S(1)} %bitcast.13, bf16[16,128,128]{2,1,0:T(8,128)(2,1)S(1)} %collective-permute-done.7.refs_0_, ...), custom_call_target="tpu_custom_call" | custom-call | flops 20000000000 | bytes 1048576 | tf_op jit(solution)/shard_map/close_sums/pallas_call | solution.py:161
  94.9 4.6 %collective-permute-start.12 = (s16[1056,128]{1,0:T(8,128)(2,1)S(1)}, s16[1056,128]{1,0:T(8,128)(2,1)S(1)}, u32[]{:S(2)}, u32[]{:S(2)}) collective-permute-start(s16[1056,128]{1,0:T(8,128)(2,1)S(1)} %get-tuple-element.43), channel_id=1, source_target_pairs={{0,256},{128,384},{256,0},{384,128},{1,257},{129,385},{257,1},{385... | collective-permute-start | bytes 811016 | tf_op jit(solution)/shard_map/ppermute | solution.py:314
  99.6 2.2 %collective-permute-start.13 = (s16[1056,128]{1,0:T(8,128)(2,1)S(1)}, s16[1056,128]{1,0:T(8,128)(2,1)S(1)}, u32[]{:S(2)}, u32[]{:S(2)}) collective-permute-start(s16[1056,128]{1,0:T(8,128)(2,1)S(1)} %get-tuple-element.44), channel_id=1, source_target_pairs={{0,128},{128,256},{256,384},{384,0},{1,129},{129,257},{257,385},{3... | collective-permute-start | bytes 811016 | tf_op jit(solution)/shard_map/ppermute | solution.py:314
  101.8 4.3 %collective-permute-start.14 = (s16[1056,128]{1,0:T(8,128)(2,1)S(1)}, s16[1056,128]{1,0:T(8,128)(2,1)S(1)}, u32[]{:S(2)}, u32[]{:S(2)}) collective-permute-start(s16[1056,128]{1,0:T(8,128)(2,1)S(1)} %get-tuple-element.45), channel_id=1, source_target_pairs={{0,384},{128,0},{256,128},{384,256},{1,385},{129,1},{257,129},{385... | collective-permute-start | bytes 811016 | tf_op jit(solution)/shard_map/ppermute | solution.py:314
  106.1 0.0 collective-permute-done.16.refs_1_
  106.1 2.4 %close_sums.3 = (f32[32,32,128]{2,1,0:T(8,128)S(1)}, s16[1056,128]{1,0:T(8,128)(2,1)S(1)}, s16[1056,128]{1,0:T(8,128)(2,1)S(1)}, s16[1056,128]{1,0:T(8,128)(2,1)S(1)}) custom-call(s32[16,128]{1,0:T(8,128)S(1)} %positions.1.place_ref, bf16[16,1552,128]{2,1,0:T(8,128)(2,1)S(1)} %bitcast.14, bf16[16,128,128]{2,1,0:T(8,128)(2,1)S(1)} %collective-permute-done.15.refs_0_, ...), custom_call_target="tpu_custom_call" | custom-call | flops 99999997952 | bytes 1048576 | tf_op jit(solution)/shard_map/close_sums/pallas_call | solution.py:161
  108.5 1.9 %collective-permute-start.17 = (s16[1056,128]{1,0:T(8,128)(2,1)S(1)}, s16[1056,128]{1,0:T(8,128)(2,1)S(1)}, u32[]{:S(2)}, u32[]{:S(2)}) collective-permute-start(s16[1056,128]{1,0:T(8,128)(2,1)S(1)} %get-tuple-element.50), channel_id=1, source_target_pairs={{0,256},{128,384},{256,0},{384,128},{1,257},{129,385},{257,1},{385... | collective-permute-start | bytes 811016 | tf_op jit(solution)/shard_map/ppermute | solution.py:314
  110.5 2.5 %collective-permute-start.18 = (s16[1056,128]{1,0:T(8,128)(2,1)S(1)}, s16[1056,128]{1,0:T(8,128)(2,1)S(1)}, u32[]{:S(2)}, u32[]{:S(2)}) collective-permute-start(s16[1056,128]{1,0:T(8,128)(2,1)S(1)} %get-tuple-element.51), channel_id=1, source_target_pairs={{0,128},{128,256},{256,384},{384,0},{1,129},{129,257},{257,385},{3... | collective-permute-start | bytes 811016 | tf_op jit(solution)/shard_map/ppermute | solution.py:314
  113.0 0.0 collective-permute-done.12.refs_0_
  113.0 4.0 %collective-permute-start.19 = (s16[1056,128]{1,0:T(8,128)(2,1)S(1)}, s16[1056,128]{1,0:T(8,128)(2,1)S(1)}, u32[]{:S(2)}, u32[]{:S(2)}) collective-permute-start(s16[1056,128]{1,0:T(8,128)(2,1)S(1)} %get-tuple-element.52), channel_id=1, source_target_pairs={{0,384},{128,0},{256,128},{384,256},{1,385},{129,1},{257,129},{385... | collective-permute-start | bytes 811016 | tf_op jit(solution)/shard_map/ppermute | solution.py:314
  117.0 0.3 first_combine.1.first_ref
  117.3 0.1 collective-permute-done.17.refs_0_
  117.4 6.5 %collective-permute-done.18.refs_1_ = s16[1056,128]{1,0:T(8,128)(2,1)S(1)} collective-permute-done((s16[1056,128]{1,0:T(8,128)(2,1)S(1)}, s16[1056,128]{1,0:T(8,128)(2,1)S(1)}, u32[]{:S(2)}, u32[]{:S(2)}) %collective-permute-start.18) | collective-permute-done | bytes 270368 | tf_op jit(solution)/shard_map/ppermute | solution.py:314
  123.8 0.0 collective-permute-done.19.refs_2_
  123.8 2.0 %last_combine.1 = f32[2048,128]{1,0:T(8,128)} custom-call(f32[32,32,128]{2,1,0:T(8,128)S(1)} %first_combine.1.first_ref, f32[32,32,128]{2,1,0:T(8,128)S(1)} %get-tuple-element.49.own_ref, s16[1056,128]{1,0:T(8,128)(2,1)S(1)} %collective-permute-done.17.refs_0_, s16[1056,128]{1,0:T(8,128)(2,1)S(1)} %collective-permute-done.18.refs_1_, ...), custom_call_target="tpu_custom_call" | custom-call | flops 1000000000 | bytes 1048576 | tf_op jit(solution)/shard_map/last_combine/pallas_call | solution.py:241
  (14 shorter events, 0.0 us)
Async XLA Ops:
  6.5 58.6 %all-gather.3.cloned.1.call-start = ((), (), s32[]{:S(2)}) async-start(), calls=%async_computation | async-start | bytes 6754304 | tf_op jit(solution)/shard_map/all_gather | solution.py:351
  10.3 23.3 %collective-permute-start.2 = (bf16[16,128,128]{2,1,0:T(8,128)(2,1)}, bf16[16,128,128]{2,1,0:T(8,128)(2,1)S(1)}, u32[]{:S(2)}, u32[]{:S(2)}) collective-permute-start(bf16[16,128,128]{2,1,0:T(8,128)(2,1)} %get-tuple-element.29.refs_4_), channel_id=1, source_target_pairs={{0,16},{16,32},{32,48},{48,64},{64,80},{80,96},{96,112},{112,0},{1... | collective-permute-start | bytes 1572872 | tf_op jit(solution)/shard_map/ppermute | solution.py:314
  15.2 20.4 %collective-permute-start.6 = (bf16[16,128,128]{2,1,0:T(8,128)(2,1)}, bf16[16,128,128]{2,1,0:T(8,128)(2,1)S(1)}, u32[]{:S(2)}, u32[]{:S(2)}) collective-permute-start(bf16[16,128,128]{2,1,0:T(8,128)(2,1)} %get-tuple-element.32.refs_5_), channel_id=1, source_target_pairs={{0,112},{16,0},{32,16},{48,32},{64,48},{80,64},{96,80},{112,96},{1... | collective-permute-start | bytes 1572872 | tf_op jit(solution)/shard_map/ppermute | solution.py:314
  23.8 22.1 %collective-permute-start = (bf16[16,128,128]{2,1,0:T(8,128)(2,1)}, bf16[16,128,128]{2,1,0:T(8,128)(2,1)}, u32[]{:S(2)}, u32[]{:S(2)}) collective-permute-start(bf16[16,128,128]{2,1,0:T(8,128)(2,1)} %get-tuple-element.29.refs_4_), channel_id=1, source_target_pairs={{0,112},{16,0},{32,16},{48,32},{64,48},{80,64},{96,80},{112,96},{1... | collective-permute-start | bytes 1572872 | tf_op jit(solution)/shard_map/ppermute | solution.py:314
  27.1 24.1 %collective-permute-start.5 = (bf16[16,128,128]{2,1,0:T(8,128)(2,1)}, bf16[16,128,128]{2,1,0:T(8,128)(2,1)S(1)}, u32[]{:S(2)}, u32[]{:S(2)}) collective-permute-start(bf16[16,128,128]{2,1,0:T(8,128)(2,1)} %get-tuple-element.32.refs_5_), channel_id=1, source_target_pairs={{0,16},{16,32},{32,48},{48,64},{64,80},{80,96},{96,112},{112,0},{1... | collective-permute-start | bytes 1572872 | tf_op jit(solution)/shard_map/ppermute | solution.py:314
  33.7 22.6 %collective-permute-start.3 = (bf16[16,128,128]{2,1,0:T(8,128)(2,1)S(1)}, bf16[16,128,128]{2,1,0:T(8,128)(2,1)S(1)}, u32[]{:S(2)}, u32[]{:S(2)}) collective-permute-start(bf16[16,128,128]{2,1,0:T(8,128)(2,1)S(1)} %collective-permute-done.2.refs_0_), channel_id=1, source_target_pairs={{0,16},{16,32},{32,48},{48,64},{64,80},{80,96},{96,112},{112,0},{1... | collective-permute-start | bytes 1572872 | tf_op jit(solution)/shard_map/ppermute | solution.py:314
  35.6 22.6 %collective-permute-start.9 = (bf16[16,128,128]{2,1,0:T(8,128)(2,1)S(1)}, bf16[16,128,128]{2,1,0:T(8,128)(2,1)}, u32[]{:S(2)}, u32[]{:S(2)}) collective-permute-start(bf16[16,128,128]{2,1,0:T(8,128)(2,1)S(1)} %collective-permute-done.6.refs_3_), channel_id=1, source_target_pairs={{0,112},{16,0},{32,16},{48,32},{64,48},{80,64},{96,80},{112,96},{1... | collective-permute-start | bytes 1572872 | tf_op jit(solution)/shard_map/ppermute | solution.py:314
  40.2 0.8 copy-start.3
  45.9 22.5 %collective-permute-start.1 = (bf16[16,128,128]{2,1,0:T(8,128)(2,1)}, bf16[16,128,128]{2,1,0:T(8,128)(2,1)S(1)}, u32[]{:S(2)}, u32[]{:S(2)}) collective-permute-start(bf16[16,128,128]{2,1,0:T(8,128)(2,1)} %collective-permute-done.refs_2_), channel_id=1, source_target_pairs={{0,112},{16,0},{32,16},{48,32},{64,48},{80,64},{96,80},{112,96},{1... | collective-permute-start | bytes 1572872 | tf_op jit(solution)/shard_map/ppermute | solution.py:314
  51.2 27.2 %collective-permute-start.11 = (bf16[16,128,128]{2,1,0:T(8,128)(2,1)S(1)}, bf16[16,128,128]{2,1,0:T(8,128)(2,1)S(1)}, u32[]{:S(2)}, u32[]{:S(2)}) collective-permute-start(bf16[16,128,128]{2,1,0:T(8,128)(2,1)S(1)} %collective-permute-done.5.refs_1_), channel_id=1, source_target_pairs={{0,16},{16,32},{32,48},{48,64},{64,80},{80,96},{96,112},{112,0},{1... | collective-permute-start | bytes 1572872 | tf_op jit(solution)/shard_map/ppermute | solution.py:314
  56.3 20.2 %collective-permute-start.4 = (bf16[16,128,128]{2,1,0:T(8,128)(2,1)S(1)}, bf16[16,128,128]{2,1,0:T(8,128)(2,1)}, u32[]{:S(2)}, u32[]{:S(2)}) collective-permute-start(bf16[16,128,128]{2,1,0:T(8,128)(2,1)S(1)} %collective-permute-done.3.refs_0_), channel_id=1, source_target_pairs={{0,16},{16,32},{32,48},{48,64},{64,80},{80,96},{96,112},{112,0},{1... | collective-permute-start | bytes 1572872 | tf_op jit(solution)/shard_map/ppermute | solution.py:314
  58.2 21.4 %collective-permute-start.10 = (bf16[16,128,128]{2,1,0:T(8,128)(2,1)}, bf16[16,128,128]{2,1,0:T(8,128)(2,1)S(1)}, u32[]{:S(2)}, u32[]{:S(2)}) collective-permute-start(bf16[16,128,128]{2,1,0:T(8,128)(2,1)} %collective-permute-done.9.refs_3_), channel_id=1, source_target_pairs={{0,112},{16,0},{32,16},{48,32},{64,48},{80,64},{96,80},{112,96},{1... | collective-permute-start | bytes 1572872 | tf_op jit(solution)/shard_map/ppermute | solution.py:314
  65.1 8.5 %copy-start = (bf16[24832,128]{1,0:T(8,128)(2,1)S(1)}, bf16[24832,128]{1,0:T(8,128)(2,1)}, u32[]{:S(2)}) copy-start(bf16[24832,128]{1,0:T(8,128)(2,1)} %all-gather.3.cloned.1.call-done) | copy-start | bytes 19070980
  65.1 8.5 %copy-start.4 = (bf16[16,128,128]{2,1,0:T(8,128)(2,1)S(1)}, bf16[16,128,128]{2,1,0:T(8,128)(2,1)}, u32[]{:S(2)}) copy-start(bf16[16,128,128]{2,1,0:T(8,128)(2,1)} %copy-done.3) | copy-start | bytes 1572868
  67.5 12.1 %copy-start.1 = (bf16[16,128,128]{2,1,0:T(8,128)(2,1)S(1)}, bf16[16,128,128]{2,1,0:T(8,128)(2,1)}, u32[]{:S(2)}) copy-start(bf16[16,128,128]{2,1,0:T(8,128)(2,1)} %get-tuple-element.29.refs_4_) | copy-start | bytes 1572868
  67.5 12.1 %copy-start.2 = (bf16[16,128,128]{2,1,0:T(8,128)(2,1)S(1)}, bf16[16,128,128]{2,1,0:T(8,128)(2,1)}, u32[]{:S(2)}) copy-start(bf16[16,128,128]{2,1,0:T(8,128)(2,1)} %get-tuple-element.32.refs_5_) | copy-start | bytes 1572868
  68.4 23.3 %collective-permute-start.8 = (bf16[16,128,128]{2,1,0:T(8,128)(2,1)S(1)}, bf16[16,128,128]{2,1,0:T(8,128)(2,1)S(1)}, u32[]{:S(2)}, u32[]{:S(2)}) collective-permute-start(bf16[16,128,128]{2,1,0:T(8,128)(2,1)S(1)} %collective-permute-done.1.refs_2_), channel_id=1, source_target_pairs={{0,112},{16,0},{32,16},{48,32},{64,48},{80,64},{96,80},{112,96},{1... | collective-permute-start | bytes 1572872 | tf_op jit(solution)/shard_map/ppermute | solution.py:314
  76.5 16.6 %collective-permute-start.7 = (bf16[16,128,128]{2,1,0:T(8,128)(2,1)}, bf16[16,128,128]{2,1,0:T(8,128)(2,1)S(1)}, u32[]{:S(2)}, u32[]{:S(2)}) collective-permute-start(bf16[16,128,128]{2,1,0:T(8,128)(2,1)} %collective-permute-done.4.refs_6_), channel_id=1, source_target_pairs={{0,16},{16,32},{32,48},{48,64},{64,80},{80,96},{96,112},{112,0},{1... | collective-permute-start | bytes 1572872 | tf_op jit(solution)/shard_map/ppermute | solution.py:314
  84.5 21.6 %collective-permute-start.15 = (bf16[16,128,128]{2,1,0:T(8,128)(2,1)S(1)}, bf16[16,128,128]{2,1,0:T(8,128)(2,1)S(1)}, u32[]{:S(2)}, u32[]{:S(2)}) collective-permute-start(bf16[16,128,128]{2,1,0:T(8,128)(2,1)S(1)} %collective-permute-done.10.refs_7_), channel_id=1, source_target_pairs={{0,112},{16,0},{32,16},{48,32},{64,48},{80,64},{96,80},{112,96},{1... | collective-permute-start | bytes 1572872 | tf_op jit(solution)/shard_map/ppermute | solution.py:314
  89.7 16.4 %collective-permute-start.16 = (bf16[16,128,128]{2,1,0:T(8,128)(2,1)S(1)}, bf16[16,128,128]{2,1,0:T(8,128)(2,1)S(1)}, u32[]{:S(2)}, u32[]{:S(2)}) collective-permute-start(bf16[16,128,128]{2,1,0:T(8,128)(2,1)S(1)} %collective-permute-done.11.refs_1_), channel_id=1, source_target_pairs={{0,16},{16,32},{32,48},{48,64},{64,80},{80,96},{96,112},{112,0},{1... | collective-permute-start | bytes 1572872 | tf_op jit(solution)/shard_map/ppermute | solution.py:314
  94.9 18.0 %collective-permute-start.12 = (s16[1056,128]{1,0:T(8,128)(2,1)S(1)}, s16[1056,128]{1,0:T(8,128)(2,1)S(1)}, u32[]{:S(2)}, u32[]{:S(2)}) collective-permute-start(s16[1056,128]{1,0:T(8,128)(2,1)S(1)} %get-tuple-element.43), channel_id=1, source_target_pairs={{0,256},{128,384},{256,0},{384,128},{1,257},{129,385},{257,1},{385... | collective-permute-start | bytes 811016 | tf_op jit(solution)/shard_map/ppermute | solution.py:314
  99.6 17.4 %collective-permute-start.13 = (s16[1056,128]{1,0:T(8,128)(2,1)S(1)}, s16[1056,128]{1,0:T(8,128)(2,1)S(1)}, u32[]{:S(2)}, u32[]{:S(2)}) collective-permute-start(s16[1056,128]{1,0:T(8,128)(2,1)S(1)} %get-tuple-element.44), channel_id=1, source_target_pairs={{0,128},{128,256},{256,384},{384,0},{1,129},{129,257},{257,385},{3... | collective-permute-start | bytes 811016 | tf_op jit(solution)/shard_map/ppermute | solution.py:314
  101.8 15.2 %collective-permute-start.14 = (s16[1056,128]{1,0:T(8,128)(2,1)S(1)}, s16[1056,128]{1,0:T(8,128)(2,1)S(1)}, u32[]{:S(2)}, u32[]{:S(2)}) collective-permute-start(s16[1056,128]{1,0:T(8,128)(2,1)S(1)} %get-tuple-element.45), channel_id=1, source_target_pairs={{0,384},{128,0},{256,128},{384,256},{1,385},{129,1},{257,129},{385... | collective-permute-start | bytes 811016 | tf_op jit(solution)/shard_map/ppermute | solution.py:314
  108.5 8.8 %collective-permute-start.17 = (s16[1056,128]{1,0:T(8,128)(2,1)S(1)}, s16[1056,128]{1,0:T(8,128)(2,1)S(1)}, u32[]{:S(2)}, u32[]{:S(2)}) collective-permute-start(s16[1056,128]{1,0:T(8,128)(2,1)S(1)} %get-tuple-element.50), channel_id=1, source_target_pairs={{0,256},{128,384},{256,0},{384,128},{1,257},{129,385},{257,1},{385... | collective-permute-start | bytes 811016 | tf_op jit(solution)/shard_map/ppermute | solution.py:314
  110.5 13.3 %collective-permute-start.18 = (s16[1056,128]{1,0:T(8,128)(2,1)S(1)}, s16[1056,128]{1,0:T(8,128)(2,1)S(1)}, u32[]{:S(2)}, u32[]{:S(2)}) collective-permute-start(s16[1056,128]{1,0:T(8,128)(2,1)S(1)} %get-tuple-element.51), channel_id=1, source_target_pairs={{0,128},{128,256},{256,384},{384,0},{1,129},{129,257},{257,385},{3... | collective-permute-start | bytes 811016 | tf_op jit(solution)/shard_map/ppermute | solution.py:314
  113.0 10.8 %collective-permute-start.19 = (s16[1056,128]{1,0:T(8,128)(2,1)S(1)}, s16[1056,128]{1,0:T(8,128)(2,1)S(1)}, u32[]{:S(2)}, u32[]{:S(2)}) collective-permute-start(s16[1056,128]{1,0:T(8,128)(2,1)S(1)} %get-tuple-element.52), channel_id=1, source_target_pairs={{0,384},{128,0},{256,128},{384,256},{1,385},{129,1},{257,129},{385... | collective-permute-start | bytes 811016 | tf_op jit(solution)/shard_map/ppermute | solution.py:314
Sparse Core Ops, SparseCore 0:
  10.5 54.5 all-gather.2
